TPU v7x, 128 devices: a whole 4x4x4 slice. The times are simulated.
128 devices in a mesh: seq: 16 (over y, x), ep: 8 (over z, core).
Axes of the slice: x: 4, y: 4, z: 4, core: 2. Of those that a mesh axis runs over, the one named last changes fastest.
Arguments:
- tokens: bfloat16 [16384, 2560], P(('seq', 'ep')), may hold values from -6 to 6
- expert_ids: int32 [16384, 6], P(('seq', 'ep')), may hold values from 0 to 23, as said below
- devices: int32 [16384, 3], P(('seq', 'ep')), may hold values from 0 to 7, as said below
- slots: int32 [16384, 3], P(('seq', 'ep')), may hold values from -1 to 11, as said below
- gates: float32 [16384, 6], P(('seq', 'ep')), may hold values from 0.05 to 0.5
- w_gate: bfloat16 [24, 2560, 2048], P('ep', None, 'seq'), may hold values from -0.125 to 0.125
- w_up: bfloat16 [24, 2560, 2048], P('ep', None, 'seq'), may hold values from -0.125 to 0.125
- w_down: bfloat16 [24, 2048, 2560], P('ep', 'seq'), may hold values from -0.125 to 0.125
- shared_gate: bfloat16 [2560, 2048], P(None, 'ep'), may hold values from -0.125 to 0.125
- shared_up: bfloat16 [2560, 2048], P(None, 'ep'), may hold values from -0.125 to 0.125
- shared_down: bfloat16 [2560, 2048], P(None, 'ep'), may hold values from -0.125 to 0.125
Outputs:
- moe_out: bfloat16 [16384, 2560], P(('seq', 'ep'))
Inputs may be any that keep to these rules, and one draw needn't show every extreme that they name: Each token names 3 different devices of ep. `expert_ids`: the 6 ids of a token differ, and id // 3 is one of the token's devices; a device of the token may hold none of them. `slots`: among the tokens of one device, taken in token order, the first 12 of those that name device d of ep get 0, 1, 2 and so on up to 11 in the matching entry; any later ones get -1 and are dropped.
All inputs are finite; a program needn't handle non-finite values.
Results may differ from a plain program's by a relative error of at most 0.018.
Values may be sent and summed in bfloat16 or wider, within the bound.
A program may use at most 192 MiB of HBM per device.

v0:
```python
import jax
import jax.numpy as jnp
from jax import lax
from jax.sharding import PartitionSpec as P


def local_gates(expert_ids, devices, gates, experts_here):
    owners = (
        devices[:, :, None] * experts_here
        + jnp.arange(experts_here, dtype=jnp.int32)[None, None, :]
    )
    matches = expert_ids[:, None, None, :] == owners[:, :, :, None]
    summed = jnp.sum(jnp.where(matches, gates[:, None, None, :], jnp.float32(0.0)), axis=3)
    return summed.astype(jnp.bfloat16)


def swiglu(inputs, gate_block, up_block):
    first = jnp.dot(inputs, gate_block, preferred_element_type=jnp.float32)
    second = jnp.dot(inputs, up_block, preferred_element_type=jnp.float32)
    return jax.nn.silu(first) * second


def local(
    tokens,
    expert_ids,
    devices,
    slots,
    gates,
    w_gate,
    w_up,
    w_down,
    shared_gate,
    shared_up,
    shared_down,
):
    expert_devices = lax.axis_size("ep")
    tok_rows, width = tokens.shape
    capacity = tok_rows * 3 // 32
    experts_here = w_gate.shape[0]
    send_count = expert_devices * capacity
    slot_gate = local_gates(expert_ids, devices, gates, experts_here)
    target = jnp.where(slots >= 0, devices * capacity + slots, -1)
    slot_ids = jnp.arange(send_count, dtype=jnp.int32)
    placing = jnp.any(slot_ids[:, None, None] == target[None, :, :], axis=2).astype(jnp.bfloat16)
    send_rows = jnp.dot(placing, tokens, preferred_element_type=jnp.float32).astype(jnp.bfloat16)
    place_full = (slot_ids[:, None, None] == target[None, :, :]).astype(jnp.float32)
    send_gate = jnp.einsum("stj,tjk->sk", place_full, slot_gate.astype(jnp.float32)).astype(
        jnp.bfloat16
    )
    send_rows = send_rows.reshape(expert_devices, capacity, width)
    send_gate = send_gate.reshape(expert_devices, capacity, experts_here)
    slot_rows, gate_rows = (
        lax.all_to_all(send_rows, "ep", split_axis=0, concat_axis=0, tiled=True),
        lax.all_to_all(send_gate, "ep", split_axis=0, concat_axis=0, tiled=True),
    )
    slot_rows, gate_rows = (
        lax.all_gather(slot_rows, "seq", axis=0, tiled=True),
        lax.all_gather(gate_rows, "seq", axis=0, tiled=True),
    )
    slot_rows = slot_rows.reshape(-1, width)
    gate_rows = gate_rows.reshape(-1, experts_here)
    inputs = slot_rows
    weights = gate_rows.astype(jnp.float32)
    running = jnp.zeros((lax.axis_size("seq") * send_count, width), jnp.float32)
    for k in range(experts_here):
        hidden = (swiglu(inputs, w_gate[k], w_up[k]) * weights[:, k : k + 1]).astype(jnp.bfloat16)
        running = running + jnp.dot(hidden, w_down[k], preferred_element_type=jnp.float32)
    slot_out = lax.psum_scatter(
        running.astype(jnp.bfloat16), "seq", scatter_dimension=0, tiled=True
    )
    returned = lax.all_to_all(
        slot_out.reshape(expert_devices, capacity, width),
        "ep",
        split_axis=0,
        concat_axis=0,
        tiled=True,
    )
    returned = returned.reshape(send_count, width)
    routed = lax.dot_general(
        placing, returned, (((0,), (0,)), ((), ())), preferred_element_type=jnp.float32
    )
    whole = lax.all_gather(tokens, "ep", axis=0, tiled=True)
    inputs = whole
    hidden = swiglu(inputs, shared_gate, shared_up).astype(jnp.bfloat16)
    shared = lax.psum_scatter(
        lax.dot_general(
            hidden, shared_down, (((1,), (1,)), ((), ())), preferred_element_type=jnp.float32
        ).astype(jnp.bfloat16),
        "ep",
        scatter_dimension=0,
        tiled=True,
    ).astype(jnp.float32)
    return (shared + routed).astype(jnp.bfloat16)


def solution(mesh):
    in_specs = (
        P(("seq", "ep"), None),
        P(("seq", "ep"), None),
        P(("seq", "ep"), None),
        P(("seq", "ep"), None),
        P(("seq", "ep"), None),
        P("ep", None, "seq"),
        P("ep", None, "seq"),
        P("ep", "seq", None),
        P(None, "ep"),
        P(None, "ep"),
        P(None, "ep"),
    )
    out_specs = P(("seq", "ep"), None)
    return jax.shard_map(local, mesh=mesh, in_specs=in_specs, out_specs=out_specs, check_vma=False)
```

profile of v0, /device:TPU:1, one launch (start us, length us, event | category | flops | bytes accessed | tf_op | source)
XLA Modules:
  0.0 325.1 jit_solution(4371557669806739475)
XLA Ops:
  6.5 0.0 copy-start
  6.5 0.0 copy-start.4
  6.5 0.0 copy-start.3
  6.5 0.0 all-gather.5.cloned.1.call-start
  6.5 0.8 broadcast_multiply_fusion
  7.4 1.4 convolution_convert_fusion.1
  8.8 0.1 reshape.26
  8.9 17.6 %all_to_all.15 = bf16[8,12,2560]{2,1,0:T(8,128)(2,1)S(1)} all-to-all(bf16[8,12,2560]{2,1,0:T(8,128)(2,1)S(1)} %reshape.26), channel_id=1, replica_groups=mesh['seq'=16,'ep'=8] {'ep'}, dimensions={0} | all-to-all | bytes 983040 | tf_op jit(solution)/shard_map/all_to_all | solution.py:53
  26.4 1.1 copy.32
  27.5 0.0 all-gather.5.cloned.1.call-update
  27.5 0.0 all-gather.3.cloned.1.call-start
  27.6 0.7 all-gather.3.cloned.1.call-update
  28.3 0.0 reduce-scatter.5.cloned.1.call-start
  28.3 0.0 copy-done.4
  28.3 0.0 copy-done.3
  28.4 0.1 fusion.10
  28.5 0.1 reshape.28
  28.6 7.8 %all_to_all.16 = bf16[8,12,3]{1,2,0:T(4,128)(2,1)S(1)} all-to-all(bf16[8,12,3]{1,2,0:T(4,128)(2,1)S(1)} %copy.34), channel_id=1, replica_groups=mesh['seq'=16,'ep'=8] {'ep'}, dimensions={0} | all-to-all | bytes 1152 | tf_op jit(solution)/shard_map/all_to_all | solution.py:54
  36.5 20.0 %all_gather.11 = bf16[128,12,3]{1,0,2:T(8,128)(2,1)S(1)} all-gather(bf16[8,12,3]{1,0,2:T(8,128)(2,1)S(1)} %copy.35), channel_id=1, replica_groups=mesh['seq'=16,'ep'=8] {'seq'}, dimensions={0}, use_global_device_ids=true | all-gather | bytes 9792 | tf_op jit(solution)/shard_map/all_gather | solution.py:58
  56.4 0.2 reshape.31
  56.6 0.1 slice_reduce_fusion
  56.6 39.2 %all-gather.5.cloned.1.call-done = bf16[128,12,2560]{2,0,1:T(8,128)(2,1)} async-done(((bf16[8,12,2560]{2,0,1:T(8,128)(2,1)}), bf16[128,12,2560]{2,0,1:T(8,128)(2,1)}) %all-gather.5.cloned.1.call-update) | async-done | bytes 7864336 | tf_op jit(solution)/shard_map/all_gather | solution.py:57
  95.9 11.7 %copy.33 = bf16[128,12,2560]{2,1,0:T(8,128)(2,1)} copy(bf16[128,12,2560]{2,0,1:T(8,128)(2,1)} %all-gather.5.cloned.1.call-done) | data formatting | bytes 15728640 | tf_op jit(solution)/shard_map/all_gather | solution.py:57
  107.6 0.0 copy-start.5
  107.6 13.1 %reshape.27 = bf16[1536,2560]{1,0:T(8,128)(2,1)} reshape(bf16[128,12,2560]{2,1,0:T(8,128)(2,1)} %copy.33) | data formatting | bytes 15728640 | tf_op jit(solution)/shard_map/reshape | solution.py:60
  120.7 0.0 copy-done.5
  120.7 6.6 %fusion.34 = f32[1536,128]{1,0:T(8,128)} fusion(bf16[1536,2560]{1,0:T(8,128)(2,1)} %reshape.27, bf16[3,2560,128]{2,1,0:T(8,128)(2,1)S(1)} %copy-done.5), kind=kOutput, calls=%fused_computation.41 | convolution fusion | flops 1006632960 | bytes 9306112 | tf_op jit(solution)/shard_map/dot_general | solution.py:18
  127.3 0.0 copy-done.1
  127.3 3.1 fusion.39
  130.4 4.3 %fusion.29 = f32[1536,128]{1,0:T(8,128)} fusion(bf16[1536,2560]{1,0:T(8,128)(2,1)S(1)} %copy-done.1, bf16[3,2560,128]{2,1,0:T(8,128)(2,1)} %param.16), kind=kOutput, calls=%fused_computation.37 | convolution fusion | flops 1006632960 | bytes 9306112 | tf_op jit(solution)/shard_map/dot_general | solution.py:18
  134.8 0.0 copy-done.2
  134.8 17.1 %fusion.7 = f32[1536,2560]{1,0:T(8,128)} fusion(bf16[1536,2560]{1,0:T(8,128)(2,1)} %reshape.27, f32[1536,128]{1,0:T(8,128)} %fusion.34, bf16[3,128,2560]{2,1,0:T(8,128)(2,1)S(1)} %copy-done.2, bf16[3,2560,128]{2,1,0:T(8,128)(2,1)} %param.17, f32[1536]{0:T(1024)S(1)} %get-tuple-element.6), kind=kOutput, calls=%fused_computation.14 | convolution fusion | flops 2014642176 | bytes 25698304 | tf_op jit(solution)/shard_map/dot_general | solution.py:67
  151.9 17.4 %fusion.8 = f32[1536,2560]{1,0:T(8,128)} fusion(bf16[1536,2560]{1,0:T(8,128)(2,1)} %reshape.27, f32[1536,128]{1,0:T(8,128)} %fusion.39, bf16[3,128,2560]{2,1,0:T(8,128)(2,1)S(1)} %copy-done.2, bf16[3,2560,128]{2,1,0:T(8,128)(2,1)} %param.17, f32[1536]{0:T(1024)S(1)} %get-tuple-element.7), kind=kOutput, calls=%fused_computation.15 | convolution fusion | flops 2014642176 | bytes 25698304 | tf_op jit(solution)/shard_map/dot_general | solution.py:67
  169.2 20.3 %add_convert_fusion = bf16[1536,2560]{1,0:T(8,128)(2,1)} fusion(f32[1536,2560]{1,0:T(8,128)} %fusion.8, f32[1536,2560]{1,0:T(8,128)} %fusion.7, bf16[1536,2560]{1,0:T(8,128)(2,1)} %reshape.27, f32[1536,128]{1,0:T(8,128)} %fusion.29, bf16[3,128,2560]{2,1,0:T(8,128)(2,1)S(1)} %copy-done.2, bf16[3,2560,128]{2,1,0:T(8,128)(2,1)} %param.17, ...), kind=kOutput, calls=%fused_computation | convolution fusion | flops 2026438656 | bytes 49291264 | tf_op jit(solution)/shard_map/dot_general | solution.py:67
  189.6 0.0 reduce-scatter.5.cloned.1.call-update
  189.6 0.3 reduce-scatter.3.cloned.1.call-start
  189.9 0.0 all-gather.3.cloned.1.call-done
  190.0 1.0 copy-done.6
  190.9 5.0 %fusion.67 = f32[1024,256]{1,0:T(8,128)} fusion(bf16[1024,2560]{1,0:T(8,128)(2,1)} %all-gather.3.cloned.1.call-done, bf16[2560,256]{1,0:T(8,128)(2,1)S(1)} %copy-done.6), kind=kOutput, calls=%fused_computation.78 | convolution fusion | flops 1342177280 | bytes 7602176 | tf_op jit(solution)/shard_map/dot_general | solution.py:18
  195.9 0.0 copy-done
  195.9 10.9 %convolution_convert_fusion = bf16[1024,2560]{1,0:T(8,128)(2,1)} fusion(bf16[2560,256]{1,0:T(8,128)(2,1)S(1)} %copy-done, bf16[1024,2560]{1,0:T(8,128)(2,1)} %all-gather.3.cloned.1.call-done, bf16[2560,256]{1,0:T(8,128)(2,1)} %param.20, f32[1024,256]{1,0:T(8,128)} %fusion.67), kind=kOutput, calls=%fused_computation.1 | convolution fusion | flops 2688548864 | bytes 14155776 | tf_op jit(solution)/shard_map/dot_general | solution.py:86
  206.7 0.0 reduce-scatter.3.cloned.1.call-update
  206.8 65.2 %reduce-scatter.5.cloned.1.call-done = bf16[96,2560]{1,0:T(8,128)(2,1)} async-done(((bf16[1536,2560]{1,0:T(8,128)(2,1)}), bf16[96,2560]{1,0:T(8,128)(2,1)}) %reduce-scatter.5.cloned.1.call-update) | async-done | bytes 491536 | tf_op jit(solution)/shard_map/reduce_scatter | solution.py:68
  272.0 1.1 reshape.29
  273.1 18.9 %all_to_all.17 = bf16[8,12,2560]{2,1,0:T(8,128)(2,1)S(1)} all-to-all(bf16[8,12,2560]{2,1,0:T(8,128)(2,1)S(1)} %reshape.29), channel_id=1, replica_groups=mesh['seq'=16,'ep'=8] {'ep'}, dimensions={0} | all-to-all | bytes 983040 | tf_op jit(solution)/shard_map/all_to_all | solution.py:71
  292.0 0.1 reshape.30
  292.1 24.2 %reduce-scatter.3.cloned.1.call-done = bf16[128,2560]{1,0:T(8,128)(2,1)} async-done(((bf16[1024,2560]{1,0:T(8,128)(2,1)}), bf16[128,2560]{1,0:T(8,128)(2,1)}) %reduce-scatter.3.cloned.1.call-update) | async-done | bytes 655376 | tf_op jit(solution)/shard_map/reduce_scatter | solution.py:85
  316.2 2.3 fusion
  (8 shorter events, 0.1 us)
Async XLA Ops:
  6.5 189.3 %copy-start = (bf16[2560,256]{1,0:T(8,128)(2,1)S(1)}, bf16[2560,256]{1,0:T(8,128)(2,1)}, u32[]{:S(2)}) copy-start(bf16[2560,256]{1,0:T(8,128)(2,1)} %param.21) | copy-start | bytes 3932164
  6.5 21.8 %copy-start.4 = (s32[128,6]{0,1:T(8,128)S(1)}, s32[128,6]{0,1:T(8,128)}, u32[]{:S(2)}) copy-start(s32[128,6]{0,1:T(8,128)} %param.12) | copy-start | bytes 9220
  6.5 21.8 %copy-start.3 = (f32[128,6]{0,1:T(8,128)S(1)}, f32[128,6]{0,1:T(8,128)}, u32[]{:S(2)}) copy-start(f32[128,6]{0,1:T(8,128)} %param.15) | copy-start | bytes 9220
  6.5 89.3 %all-gather.5.cloned.1.call-start = ((), (), s32[]{:S(2)}) async-start(), calls=%async_computation.7 | async-start | bytes 8355840 | tf_op jit(solution)/shard_map/all_gather | solution.py:57
  27.5 162.4 %all-gather.3.cloned.1.call-start = ((), (), s32[]{:S(2)}) async-start(), calls=%async_computation.5 | async-start | bytes 5898240 | tf_op jit(solution)/shard_map/all_gather | solution.py:82
  28.3 243.7 %reduce-scatter.5.cloned.1.call-start = ((), (), s32[]{:S(2)}) async-start(), calls=%async_computation.8 | async-start | bytes 8355840 | tf_op jit(solution)/shard_map/reduce_scatter | solution.py:68
  107.6 13.1 %copy-start.5 = (bf16[3,2560,128]{2,1,0:T(8,128)(2,1)S(1)}, bf16[3,2560,128]{2,1,0:T(8,128)(2,1)}, u32[]{:S(2)}) copy-start(bf16[3,2560,128]{2,1,0:T(8,128)(2,1)} %param.16) | copy-start | bytes 5898244
  120.7 6.6 %copy-start.1 = (bf16[1536,2560]{1,0:T(8,128)(2,1)S(1)}, bf16[1536,2560]{1,0:T(8,128)(2,1)}, u32[]{:S(2)}) copy-start(bf16[1536,2560]{1,0:T(8,128)(2,1)} %reshape.27) | copy-start | bytes 23592964
  130.4 4.3 %copy-start.2 = (bf16[3,128,2560]{2,1,0:T(8,128)(2,1)S(1)}, bf16[3,128,2560]{2,1,0:T(8,128)(2,1)}, u32[]{:S(2)}) copy-start(bf16[3,128,2560]{2,1,0:T(8,128)(2,1)} %param.18) | copy-start | bytes 5898244
  189.6 1.3 copy-start.6
  189.6 126.6 %reduce-scatter.3.cloned.1.call-start = ((), (), s32[]{:S(2)}) async-start(), calls=%async_computation.6 | async-start | bytes 5898240 | tf_op jit(solution)/shard_map/reduce_scatter | solution.py:85
Sparse Core Ops, SparseCore 0:
  27.6 68.1 all-gather.4
  97.6 36.8 all-gather.2
  189.7 82.1 reduce-scatter.4
  274.4 41.8 reduce-scatter.2
where the time goes:
time: 327 us; the launch traced here: 325 us
  waiting for transfers between devices  129 us (39%)
  matrix products  88.5 us (27%)
  blocking collectives  64.2 us (20%)
  local copies, waits for them, and re-layouts  28.5 us (9%)
  between operations  13.2 us (4%)
    reduce_scatter x1, waiting for transfers between devices, local(): lax.psum_scatter(running.astype(jnp.bfloat16), 'seq', scatter_dimension=0...  65.2 us
    dot_general x3, matrix products, local(): jnp.dot(hidden, w_down[k], preferred_element_type=jnp.float32)  54.8 us
    all_gather x1, waiting for transfers between devices, local(): lax.all_gather(slot_rows, 'seq', axis=0, tiled=True)  39.2 us
    reduce_scatter x1, waiting for transfers between devices, local(): lax.psum_scatter(lax.dot_general(hidden, shared_down, (((1,), (1,)), ((),...  24.2 us
    all_gather x1, blocking collectives, local(): lax.all_gather(gate_rows, 'seq', axis=0, tiled=True)  20 us
    dot_general x4, matrix products, swiglu(): first = jnp.dot(inputs, gate_block, preferred_element_type=jnp.float32)  19 us
    all_to_all x1, blocking collectives, local(): lax.all_to_all(slot_out.reshape(expert_devices, capacity, width), 'ep', s...  18.9 us
    all_to_all x1, blocking collectives, local(): lax.all_to_all(send_rows, 'ep', split_axis=0, concat_axis=0, tiled=True)  17.6 us
  transfers between devices with their start and end apart: 4, of which 3 were waited for; matrix products, arithmetic and copies ran while one was open for 34% of the time, Pallas kernels for 0%

commit v1 on v0

v1 whole, which is shorter than its diff:
```python
import functools

import jax
import jax.numpy as jnp
from jax import lax
from jax.experimental import pallas as pl
from jax.experimental.pallas import tpu as pltpu
from jax.sharding import PartitionSpec as P

MESH = pl.DeviceIdType.MESH
F32 = jnp.float32
BF16 = jnp.bfloat16

SIDE = 4
N_EP = 8
TOK = 128
D = 2560
WIDE = D + 128
CAP = 12
PIECE = 16
HALF = 4 * CAP
SH = 256
LEFT = 1280

HERE, NEXT, PREV, FAR = 0, 1, 2, 3


class Copies:
    def __init__(self, send, recv):
        self.send, self.recv, self.made = send, recv, []

    def start(self, src, dst, device):
        i = len(self.made)
        copy = pltpu.make_async_remote_copy(
            src_ref=src,
            dst_ref=dst,
            send_sem=self.send.at[i],
            recv_sem=self.recv.at[i],
            device_id=device,
            device_id_type=MESH,
        )
        copy.start()
        self.made.append(copy)
        return copy


def add_rows(dst, start, rows, cols, terms):
    @pl.loop(0, rows // 16)
    def _(i):
        at = pl.ds(pl.multiple_of(start + i * 16, 16), 16)
        total = dst[at, cols].astype(F32)
        for ref, first in terms:
            total += ref[pl.ds(pl.multiple_of(first + i * 16, 16), 16), cols].astype(F32)
        dst[at, cols] = total.astype(BF16)


def row(b, h, a):
    return ((b * 2 + h) * 4 + a) * HALF


def kernel(
    ids_ref,
    dev_ref,
    slot_ref,
    gates_ref,
    tok_hbm,
    wg_hbm,
    wu_hbm,
    wd_hbm,
    sg_hbm,
    su_hbm,
    sd_hbm,
    out_ref,
    wgu,
    wd,
    sgu,
    sd,
    send,
    land,
    xs,
    ys,
    hid,
    r1,
    r2,
    t1,
    t2,
    back,
    ret,
    shx,
    shp,
    shh,
    sib,
    u1,
    u2,
    send_sem,
    recv_sem,
    local_sem,
):
    seq, ep = lax.axis_index("seq"), lax.axis_index("ep")
    y, x = seq // SIDE, lax.rem(seq, SIDE)
    z, core = ep // 2, lax.rem(ep, 2)

    def up(v, by):
        return lax.rem(v + by, SIDE)

    xp, xm = (y * SIDE + up(x, 1), ep), (y * SIDE + up(x, 3), ep)
    yp, ym = (up(y, 1) * SIDE + x, ep), (up(y, 3) * SIDE + x, ep)
    zp, zm = (seq, up(z, 1) * 2 + core), (seq, up(z, 3) * 2 + core)
    twin = (seq, z * 2 + 1 - core)
    ep_to = [(seq, lax.rem(ep + r, N_EP)) for r in range(N_EP)]
    ep_from = [(seq, lax.rem(ep + N_EP - r, N_EP)) for r in range(N_EP)]
    rings = [((xp, xm), (yp, ym)), ((yp, ym), (xp, xm))]

    barrier = pltpu.get_barrier_semaphore()
    partners = [xp, xm, yp, ym] + ep_to[1:]
    for device in partners:
        pl.semaphore_signal(barrier, inc=1, device_id=device, device_id_type=MESH)

    loads = []

    def load(src, dst):
        copy = pltpu.make_async_copy(src, dst, local_sem.at[len(loads)])
        copy.start()
        loads.append(copy)
        return copy

    tok = shx.at[pl.ds(0, TOK)]
    load_tok = load(tok_hbm, tok)
    load_routed = []
    for k in range(3):
        load_routed.append(load(wg_hbm.at[k], wgu.at[k, :, pl.ds(0, 128)]))
        load_routed.append(load(wu_hbm.at[k], wgu.at[k, :, pl.ds(128, 128)]))
        load_routed.append(load(wd_hbm.at[k], wd.at[pl.ds(k * 128, 128)]))
    load_shared = [
        load(sg_hbm, sgu.at[:, pl.ds(0, SH)]),
        load(su_hbm, sgu.at[:, pl.ds(SH, SH)]),
        load(sd_hbm, sd),
    ]

    rows_i = lax.broadcasted_iota(jnp.int32, (TOK, TOK), 0)
    lanes_i = lax.broadcasted_iota(jnp.int32, (TOK, TOK), 1)
    place = jnp.zeros((TOK, TOK), F32)
    gate_of = [jnp.zeros((TOK, TOK), F32) for _ in range(3)]
    for j in range(3):
        dev = dev_ref[j : j + 1, :]
        slot = slot_ref[j : j + 1, :]
        turn = dev - ep
        turn = jnp.where(turn < 0, turn + N_EP, turn)
        target = jnp.where(slot >= 0, turn * PIECE + slot, -1)
        hit = rows_i == target
        place = jnp.where(hit, 1.0, place)
        for k in range(3):
            summed = jnp.zeros((1, TOK), F32)
            for r in range(6):
                summed += jnp.where(
                    ids_ref[r : r + 1, :] == dev * 3 + k, gates_ref[r : r + 1, :], 0.0
                )
            gate_of[k] = jnp.where(hit, summed, gate_of[k])
    place = place.astype(BF16)
    columns = jnp.zeros((TOK, TOK), F32)
    for k in range(3):
        column = jnp.sum(gate_of[k], axis=1, keepdims=True)
        columns = jnp.where(lanes_i == k, column, columns)
    send[:, D:] = columns.astype(BF16)

    load_tok.wait()
    for n in range(D // 512):
        cols = slice(n * 512, (n + 1) * 512)
        send[:, cols] = jnp.dot(place, shx[0:TOK, cols], preferred_element_type=F32).astype(BF16)

    pl.semaphore_wait(barrier, len(partners))
    copies = Copies(send_sem, recv_sem)

    arrive = [None] + [
        copies.start(
            send.at[pl.ds(r * PIECE, PIECE)], land.at[pl.ds(r * PIECE, PIECE)], ep_to[r]
        )
        for r in range(1, N_EP)
    ]
    land[0:PIECE, :] = send[0:PIECE, :]

    def dense(rows, cols, flip):
        one = lax.broadcasted_iota(jnp.int32, (rows, cols), 1 if flip else 0)
        two = lax.broadcasted_iota(jnp.int32, (rows, cols), 0 if flip else 1)
        hit = jnp.zeros((rows, cols), F32)
        for i in range(4):
            inside = (one >= CAP * i) & (one < CAP * (i + 1)) & (two == one + (PIECE - CAP) * i)
            hit = jnp.where(inside, 1.0, hit)
        return hit.astype(BF16)

    squeeze = dense(HALF, 4 * PIECE, False)
    spread = dense(4 * PIECE, HALF, True)

    def xb(b, h, a, n=1):
        return xs.at[pl.ds(row(b, h, a), n * HALF)]

    def yb(b, h, a, n=1):
        return ys.at[pl.ds(row(b, h, a), n * HALF)]

    gather = [[], []]
    for h in range(2):
        for r in range(4 * h, 4 * h + 4):
            if r:
                arrive[r].wait_recv()
        for n in range(WIDE // 384):
            cols = slice(n * 384, (n + 1) * 384)
            xs[row(HERE, h, HERE) : row(HERE, h, HERE) + HALF, cols] = jnp.dot(
                squeeze, land[h * 64 : h * 64 + 64, cols], preferred_element_type=F32
            ).astype(BF16)
        (ap, am), (bp, bm) = rings[h]
        own = xb(HERE, h, HERE)
        gather[h] += [
            copies.start(own, xb(HERE, h, PREV), ap),
            copies.start(own, xb(HERE, h, NEXT), am),
            copies.start(own, xb(PREV, h, HERE), bp),
            copies.start(own, xb(NEXT, h, HERE), bm),
        ]

    def sx(dz, c):
        return shx.at[pl.ds((c * 4 + dz) * TOK, TOK)]

    lo, hi = pl.ds(0, LEFT), pl.ds(LEFT, D - LEFT)
    wide_hi = pl.ds(LEFT, WIDE - LEFT)
    ring = [
        copies.start(sx(HERE, 0), sx(PREV, 0), zp),
        copies.start(sx(HERE, 0), sx(NEXT, 0), zm),
    ]
    to_twin = [copies.start(sx(HERE, 0), sx(HERE, 1), twin)]

    def part(ref, cols):
        return ref.at[:, cols]

    for h in range(2):
        (ap, am), (bp, bm) = rings[h]
        c = gather[h]
        c[0].wait_recv()
        c.append(copies.start(part(xb(HERE, h, PREV), lo), part(xb(HERE, h, FAR), lo), ap))
        c[1].wait_recv()
        c.append(
            copies.start(part(xb(HERE, h, NEXT), wide_hi), part(xb(HERE, h, FAR), wide_hi), am)
        )
        c.append(copies.start(xb(HERE, h, PREV), xb(PREV, h, PREV), bp))
        c.append(copies.start(xb(HERE, h, PREV), xb(NEXT, h, PREV), bm))
        c.append(copies.start(xb(HERE, h, NEXT), xb(PREV, h, NEXT), bp))
        c.append(copies.start(xb(HERE, h, NEXT), xb(NEXT, h, NEXT), bm))
    for h in range(2):
        (ap, am), (bp, bm) = rings[h]
        c = gather[h]
        c[2].wait_recv()
        c.append(None)
        c.append(None)
        c.append(copies.start(xb(PREV, h, HERE), xb(FAR, h, HERE), bp))
        c[4].wait_recv()
        c[5].wait_recv()
        c[10] = copies.start(xb(HERE, h, FAR), xb(PREV, h, FAR), bp)
        c[11] = copies.start(xb(HERE, h, FAR), xb(NEXT, h, FAR), bm)
    for h in range(2):
        (ap, am), (bp, bm) = rings[h]
        c = gather[h]
        c[8].wait_recv()
        c.append(copies.start(xb(PREV, h, NEXT), xb(FAR, h, NEXT), bp))
        c[7].wait_recv()
        c.append(copies.start(xb(NEXT, h, PREV), xb(FAR, h, PREV), bm))

    def forward_tokens():
        ring[0].wait_recv()
        ring.append(copies.start(part(sx(PREV, 0), lo), part(sx(FAR, 0), lo), zp))
        to_twin.append(copies.start(sx(PREV, 0), sx(PREV, 1), twin))
        ring[1].wait_recv()
        ring.append(copies.start(part(sx(NEXT, 0), hi), part(sx(FAR, 0), hi), zm))
        to_twin.append(copies.start(sx(NEXT, 0), sx(NEXT, 1), twin))

    def routed(b):
        at = pl.ds(row(b, 0, 0), 8 * HALF)
        gate = xs[at, D:].astype(F32)
        for k in range(3):
            both = jnp.dot(xs[at, 0:D], wgu[k], preferred_element_type=F32)
            value = jax.nn.silu(both[:, :128]) * both[:, 128:] * gate[:, k : k + 1]
            hid[:, k * 128 : (k + 1) * 128] = value.astype(BF16)

        @pl.loop(0, D // 512)
        def _(n):
            cols = pl.ds(pl.multiple_of(n * 512, 512), 512)
            ys[at, cols] = jnp.dot(hid[...], wd[:, cols], preferred_element_type=F32).astype(BF16)

    forward_tokens()
    for copy in load_routed:
        copy.wait()
    routed(HERE)
    for h in range(2):
        (ap, am), (bp, bm) = rings[h]
        c = gather[h]
        c[11].wait_recv()
        c.append(copies.start(xb(NEXT, h, FAR), xb(FAR, h, FAR), bm))
    for h in range(2):
        c = gather[h]
        for i in (6, 10, 3, 9):
            c[i].wait_recv()
    routed(PREV)
    reduce = [[None] * 10, [None] * 10]
    for h in range(2):
        (ap, am), (bp, bm) = rings[h]
        reduce[h][3] = copies.start(yb(PREV, h, HERE, 2), r2.at[h, 1, pl.ds(0, 2 * HALF)], bm)
    routed(NEXT)
    for h in range(2):
        (ap, am), (bp, bm) = rings[h]
        reduce[h][2] = copies.start(
            yb(NEXT, h, PREV, 2), r2.at[h, 0, pl.ds(2 * HALF, 2 * HALF)], bp
        )

    ring[2].wait_recv()
    ring[3].wait_recv()
    to_twin.append(copies.start(sx(FAR, 0), sx(FAR, 1), twin))
    for copy in load_shared:
        copy.wait()

    def shared(c):
        @pl.loop(0, 2)
        def _(i):
            at = pl.ds(pl.multiple_of(c * 4 * TOK + i * 2 * TOK, 2 * TOK), 2 * TOK)
            both = jnp.dot(shx[at, :], sgu[...], preferred_element_type=F32)
            shh[...] = (jax.nn.silu(both[:, :SH]) * both[:, SH:]).astype(BF16)

            @pl.loop(0, D // 512)
            def _(n):
                cols = pl.ds(pl.multiple_of(n * 512, 512), 512)
                shp[at, cols] = lax.dot_general(
                    shh[...], sd[cols, :], (((1,), (1,)), ((), ())), preferred_element_type=F32
                ).astype(BF16)

    for h in range(2):
        for i in range(12, 16):
            gather[h][i].wait_recv()
    routed(FAR)
    for h in range(2):
        (ap, am), (bp, bm) = rings[h]
        reduce[h][0] = copies.start(yb(FAR, h, HERE, 2), r1.at[h, 0], bp)
        reduce[h][1] = copies.start(yb(FAR, h, PREV, 2), r1.at[h, 1], bm)

    for copy in to_twin:
        copy.wait_recv()
    shared(1)
    sums = [
        copies.start(
            shp.at[pl.ds((4 + dz) * TOK, TOK)], sib.at[pl.ds(dz * TOK, TOK)], twin
        )
        for dz in range(4)
    ]
    every = pl.ds(0, D)
    for h in range(2):
        (ap, am), (bp, bm) = rings[h]
        c = reduce[h]
        c[0].wait_recv()
        add_rows(ys, row(NEXT, h, HERE), 2 * HALF, every, [(r1.at[h, 0], 0)])
        c[4] = copies.start(yb(NEXT, h, HERE, 2), r2.at[h, 0, pl.ds(0, 2 * HALF)], bp)
        c[1].wait_recv()
        add_rows(ys, row(PREV, h, PREV), 2 * HALF, every, [(r1.at[h, 1], 0)])
        c[5] = copies.start(yb(PREV, h, PREV, 2), r2.at[h, 1, pl.ds(2 * HALF, 2 * HALF)], bm)
    shared(0)
    for copy in sums:
        copy.wait_recv()
    add_rows(shp, 0, 4 * TOK, every, [(sib, 0)])

    def sp(dz):
        return shp.at[pl.ds(dz * TOK, TOK)]

    zs = [
        copies.start(part(sp(FAR), lo), part(u1, lo), zp),
        copies.start(part(sp(FAR), hi), part(u1, hi), zm),
    ]
    zs[0].wait_recv()
    add_rows(shp, NEXT * TOK, TOK, lo, [(u1, 0)])
    zs.append(copies.start(sp(NEXT), u2.at[0], zp))
    zs[1].wait_recv()
    add_rows(shp, PREV * TOK, TOK, hi, [(u1, 0)])
    zs.append(copies.start(sp(PREV), u2.at[1], zm))

    for h in range(2):
        (ap, am), (bp, bm) = rings[h]
        c = reduce[h]
        for i in (2, 3, 4, 5):
            c[i].wait_recv()
        add_rows(
            ys,
            row(HERE, h, HERE),
            4 * HALF,
            every,
            [(r2.at[h, 0], 0), (r2.at[h, 1], 0)],
        )
        c[6] = copies.start(part(yb(HERE, h, FAR), lo), part(t1.at[h], lo), ap)
        c[7] = copies.start(part(yb(HERE, h, FAR), hi), part(t1.at[h], hi), am)
    for h in range(2):
        (ap, am), (bp, bm) = rings[h]
        c = reduce[h]
        c[6].wait_recv()
        add_rows(ys, row(HERE, h, NEXT), HALF, lo, [(t1.at[h], 0)])
        c[8] = copies.start(yb(HERE, h, NEXT), t2.at[h, 0], ap)
        c[7].wait_recv()
        add_rows(ys, row(HERE, h, PREV), HALF, hi, [(t1.at[h], 0)])
        c[9] = copies.start(yb(HERE, h, PREV), t2.at[h, 1], am)

    home = []
    for h in range(2):
        c = reduce[h]
        c[8].wait_recv()
        c[9].wait_recv()
        first = row(HERE, h, HERE)
        add_rows(ys, first, HALF, every, [(t2.at[h, 0], 0), (t2.at[h, 1], 0)])
        for n in range(D // 512):
            cols = slice(n * 512, (n + 1) * 512)
            back[h * 64 : h * 64 + 64, cols] = jnp.dot(
                spread, ys[first : first + HALF, cols], preferred_element_type=F32
            ).astype(BF16)
        for r in range(4 * h, 4 * h + 4):
            piece = pl.ds(r * PIECE, PIECE)
            if r:
                home.append(copies.start(back.at[piece], ret.at[piece], ep_from[r]))
            else:
                ret[piece, :] = back[piece, :]

    for copy in zs[2:]:
        copy.wait_recv()
    for copy in home:
        copy.wait_recv()
    for n in range(D // 512):
        cols = slice(n * 512, (n + 1) * 512)
        total = lax.dot_general(
            place, ret[:, cols], (((0,), (0,)), ((), ())), preferred_element_type=F32
        )
        total += shp[0:TOK, cols].astype(F32)
        total += u2[0, :, cols].astype(F32) + u2[1, :, cols].astype(F32)
        out_ref[:, cols] = total.astype(BF16)

    for copy in copies.made:
        copy.wait_send()


def local(
    tokens,
    expert_ids,
    devices,
    slots,
    gates,
    w_gate,
    w_up,
    w_down,
    shared_gate,
    shared_up,
    shared_down,
):
    vmem = pl.BlockSpec(memory_space=pltpu.VMEM)
    anywhere = pl.BlockSpec(memory_space=pl.ANY)
    copies = 7 + 32 + 4 + 4 + 20 + 4 + 4 + 7
    return pl.pallas_call(
        kernel,
        out_shape=jax.ShapeDtypeStruct((TOK, D), BF16),
        in_specs=[vmem] * 4 + [anywhere] * 7,
        out_specs=vmem,
        scratch_shapes=[
            pltpu.VMEM((3, D, 256), BF16),
            pltpu.VMEM((384, D), BF16),
            pltpu.VMEM((D, 2 * SH), BF16),
            pltpu.VMEM((D, SH), BF16),
            pltpu.VMEM((TOK, WIDE), BF16),
            pltpu.VMEM((TOK, WIDE), BF16),
            pltpu.VMEM((32 * HALF, WIDE), BF16),
            pltpu.VMEM((32 * HALF, D), BF16),
            pltpu.VMEM((8 * HALF, 384), BF16),
            pltpu.VMEM((2, 2, 2 * HALF, D), BF16),
            pltpu.VMEM((2, 2, 4 * HALF, D), BF16),
            pltpu.VMEM((2, HALF, D), BF16),
            pltpu.VMEM((2, 2, HALF, D), BF16),
            pltpu.VMEM((TOK, D), BF16),
            pltpu.VMEM((TOK, D), BF16),
            pltpu.VMEM((8 * TOK, D), BF16),
            pltpu.VMEM((8 * TOK, D), BF16),
            pltpu.VMEM((2 * TOK, SH), BF16),
            pltpu.VMEM((4 * TOK, D), BF16),
            pltpu.VMEM((TOK, D), BF16),
            pltpu.VMEM((2, TOK, D), BF16),
            pltpu.SemaphoreType.DMA((copies,)),
            pltpu.SemaphoreType.DMA((copies,)),
            pltpu.SemaphoreType.DMA((16,)),
        ],
        compiler_params=pltpu.CompilerParams(
            collective_id=0, has_side_effects=True, vmem_limit_bytes=62 * 1024 * 1024
        ),
        cost_estimate=pl.CostEstimate(
            flops=13_100_000_000, bytes_accessed=12_000_000, transcendentals=900_000
        ),
    )(
        expert_ids.T,
        devices.T,
        slots.T,
        gates.T,
        tokens,
        w_gate,
        w_up,
        w_down,
        shared_gate,
        shared_up,
        shared_down,
    )


def solution(mesh):
    in_specs = (
        P(("seq", "ep"), None),
        P(("seq", "ep"), None),
        P(("seq", "ep"), None),
        P(("seq", "ep"), None),
        P(("seq", "ep"), None),
        P("ep", None, "seq"),
        P("ep", None, "seq"),
        P("ep", "seq", None),
        P(None, "ep"),
        P(None, "ep"),
        P(None, "ep"),
    )
    out_specs = P(("seq", "ep"), None)
    return jax.shard_map(local, mesh=mesh, in_specs=in_specs, out_specs=out_specs, check_vma=False)
```

time: 327 us -> 126 us (0.39)
  the two profiles are of different devices: /device:TPU:1 before, /device:TPU:36 now
where the time goes in v1:
time: 126 us
  Pallas kernels  124 us (98%)
  local copies, waits for them, and re-layouts  1.97 us (2%)
    pallas_call x1, Pallas kernels, local(): pl.pallas_call(kernel, out_shape=jax.ShapeDtypeStruct((TOK, D), BF16), in...  124 us

profile of v1, /device:TPU:36, one launch (start us, length us, event | category | flops | bytes accessed | tf_op | source)
XLA Modules:
  0.0 125.8 jit_solution(10211427212985424612)
XLA Ops:
  0.0 123.8 %shard_map.109 = bf16[128,2560]{1,0:T(8,128)(2,1)} custom-call(s32[6,128]{1,0:T(8,128)} %bitcast.4, s32[3,128]{1,0:T(4,128)} %bitcast.6, s32[3,128]{1,0:T(4,128)} %bitcast.7, f32[6,128]{1,0:T(8,128)} %bitcast.5, bf16[128,2560]{1,0:T(8,128)(2,1)} %tok_hbm.1, bf16[3,2560,128]{2,1,0:T(8,128)(2,1)} %wg_hbm.1, bf16[3,2560,128]{2,1,0:T(8,128)(2,1)} %wu_hbm.1, ...), custom_call_target="tpu_custom_call" | custom-call | flops 13100000256 | bytes 12000000 | tf_op jit(solution)/shard_map/pallas_call | solution.py:454
  123.8 2.0 %copy.13 = bf16[128,2560]{1,0:T(8,128)(2,1)} copy(bf16[128,2560]{1,0:T(8,128)(2,1)} %shard_map.109) | data formatting | bytes 1310720

commit v2 on v1

v2 whole, which is shorter than its diff:
```python
import functools

import jax
import jax.numpy as jnp
from jax import lax
from jax.experimental import pallas as pl
from jax.experimental.pallas import tpu as pltpu
from jax.sharding import PartitionSpec as P

MESH = pl.DeviceIdType.MESH
F32 = jnp.float32
BF16 = jnp.bfloat16

SIDE = 4
N_EP = 8
TOK = 128
D = 2560
WIDE = D + 128
CAP = 12
PIECE = 16
HALF = 4 * CAP
SH = 256
LEFT = 1280
MAIN = 1920
TAIL = D - MAIN
ORDER = (0, 1, 2, 7, 6, 3, 4, 5)

HERE, NEXT, PREV, FAR = 0, 1, 2, 3


class Copies:
    def __init__(self, send, recv):
        self.send, self.recv, self.made = send, recv, []

    def start(self, src, dst, device):
        i = len(self.made)
        copy = pltpu.make_async_remote_copy(
            src_ref=src,
            dst_ref=dst,
            send_sem=self.send.at[i],
            recv_sem=self.recv.at[i],
            device_id=device,
            device_id_type=MESH,
        )
        copy.start()
        self.made.append(copy)
        return copy


def add_rows(dst, start, rows, cols, terms):
    @pl.loop(0, rows // 16)
    def _(i):
        at = pl.ds(pl.multiple_of(start + i * 16, 16), 16)
        total = dst[at, cols].astype(F32)
        for ref, first in terms:
            total += ref[pl.ds(pl.multiple_of(first + i * 16, 16), 16), cols].astype(F32)
        dst[at, cols] = total.astype(BF16)


def row(b, h, a):
    return ((b * 2 + h) * 4 + a) * HALF


def kernel(
    ids_ref,
    dev_ref,
    slot_ref,
    gates_ref,
    tok_hbm,
    wg_hbm,
    wu_hbm,
    wd_hbm,
    sg_hbm,
    su_hbm,
    sd_hbm,
    out_ref,
    wgu,
    wd,
    sgu,
    sd,
    send,
    land,
    xs,
    ys,
    hid,
    r1,
    ahead,
    behind,
    t1,
    tahead,
    tbehind,
    back,
    ret,
    shx,
    shp,
    shh,
    sib,
    u1,
    u2,
    send_sem,
    recv_sem,
    local_sem,
):
    seq, ep = lax.axis_index("seq"), lax.axis_index("ep")
    y, x = seq // SIDE, lax.rem(seq, SIDE)
    z, core = ep // 2, lax.rem(ep, 2)

    def up(v, by):
        return lax.rem(v + by, SIDE)

    xp, xm = (y * SIDE + up(x, 1), ep), (y * SIDE + up(x, 3), ep)
    yp, ym = (up(y, 1) * SIDE + x, ep), (up(y, 3) * SIDE + x, ep)
    zp, zm = (seq, up(z, 1) * 2 + core), (seq, up(z, 3) * 2 + core)
    twin = (seq, z * 2 + 1 - core)
    ep_to = [(seq, lax.rem(ep + r, N_EP)) for r in range(N_EP)]
    ep_from = [(seq, lax.rem(ep + N_EP - r, N_EP)) for r in range(N_EP)]
    rings = [((xp, xm), (yp, ym)), ((yp, ym), (xp, xm))]

    barrier = pltpu.get_barrier_semaphore()
    partners = [xp, xm, yp, ym] + ep_to[1:]
    for device in partners:
        pl.semaphore_signal(barrier, inc=1, device_id=device, device_id_type=MESH)

    loads = []

    def load(src, dst):
        copy = pltpu.make_async_copy(src, dst, local_sem.at[len(loads)])
        copy.start()
        loads.append(copy)
        return copy

    tok = shx.at[pl.ds(0, TOK)]
    load_tok = load(tok_hbm, tok)
    load_routed = []
    for k in range(3):
        load_routed.append(load(wg_hbm.at[k], wgu.at[k, :, pl.ds(0, 128)]))
        load_routed.append(load(wu_hbm.at[k], wgu.at[k, :, pl.ds(128, 128)]))
        load_routed.append(load(wd_hbm.at[k], wd.at[pl.ds(k * 128, 128)]))
    load_shared = [
        load(sg_hbm, sgu.at[:, pl.ds(0, SH)]),
        load(su_hbm, sgu.at[:, pl.ds(SH, SH)]),
        load(sd_hbm, sd),
    ]

    rows_i = lax.broadcasted_iota(jnp.int32, (TOK, TOK), 0)
    lanes_i = lax.broadcasted_iota(jnp.int32, (TOK, TOK), 1)
    place = jnp.zeros((TOK, TOK), F32)
    place_tail = [jnp.zeros((TOK, TOK), F32) for _ in range(3)]
    gate_of = [jnp.zeros((TOK, TOK), F32) for _ in range(3)]
    for j in range(3):
        dev = dev_ref[j : j + 1, :]
        slot = slot_ref[j : j + 1, :]
        turn = dev - ep
        turn = jnp.where(turn < 0, turn + N_EP, turn)
        piece = jnp.where(turn < 3, turn, jnp.where(turn < 6, turn + 2, 10 - turn))
        hit = rows_i == jnp.where(slot >= 0, piece * PIECE + slot, -1)
        place = jnp.where(hit, 1.0, place)
        for g in range(3):
            mine = (slot >= 4 * g) & (slot < 4 * g + 4)
            tail_row = jnp.where(mine, piece * PIECE + CAP - 4 * g + slot, -1)
            place_tail[g] = jnp.where(rows_i == tail_row, 1.0, place_tail[g])
        for k in range(3):
            summed = jnp.zeros((1, TOK), F32)
            for r in range(6):
                summed += jnp.where(
                    ids_ref[r : r + 1, :] == dev * 3 + k, gates_ref[r : r + 1, :], 0.0
                )
            gate_of[k] = jnp.where(hit, summed, gate_of[k])
    place = place.astype(BF16)
    place_tail = [p.astype(BF16) for p in place_tail]
    columns = jnp.zeros((TOK, TOK), F32)
    for k in range(3):
        column = jnp.sum(gate_of[k], axis=1, keepdims=True)
        columns = jnp.where(lanes_i == k, column, columns)
    send[:, MAIN:] = columns.astype(BF16)

    load_tok.wait()
    for g in range(3):
        cols = slice(g * TAIL, (g + 1) * TAIL)
        send[:, cols] = (
            jnp.dot(place, shx[0:TOK, cols], preferred_element_type=F32)
            + jnp.dot(place_tail[g], shx[0:TOK, MAIN:], preferred_element_type=F32)
        ).astype(BF16)

    pl.semaphore_wait(barrier, len(partners))
    copies = Copies(send_sem, recv_sem)

    arrive = [None]
    for p in range(1, N_EP):
        piece = pl.ds(p * PIECE, PIECE)
        arrive.append(copies.start(send.at[piece], land.at[piece], ep_to[ORDER[p]]))
    land[0:PIECE, :] = send[0:PIECE, :]

    def dense(flip, g=None):
        shape = (4 * PIECE, HALF) if flip else (HALF, 4 * PIECE)
        one = lax.broadcasted_iota(jnp.int32, shape, 1 if flip else 0)
        two = lax.broadcasted_iota(jnp.int32, shape, 0 if flip else 1)
        hit = jnp.zeros(shape, F32)
        for i in range(4):
            first, count, shift = CAP * i, CAP, (PIECE - CAP) * i
            if g is not None:
                first, count, shift = first + 4 * g, 4, shift + CAP - 4 * g
            inside = (one >= first) & (one < first + count) & (two == one + shift)
            hit = jnp.where(inside, 1.0, hit)
        return hit.astype(BF16)

    squeeze, squeeze_tail = dense(False), [dense(False, g) for g in range(3)]
    spread, spread_tail = dense(True), [dense(True, g) for g in range(3)]

    lo, hi = pl.ds(0, LEFT), pl.ds(LEFT, D - LEFT)
    wide_hi = pl.ds(LEFT, WIDE - LEFT)

    def xb(b, h, a, cols):
        return xs.at[pl.ds(row(b, h, a), HALF), cols]

    streams = []
    for h in range(2):
        (ap, am), (bp, bm) = rings[h]
        streams.append((h, lo, lo, PREV, NEXT, ap, am, bp, bm))
        streams.append((h, wide_hi, hi, NEXT, PREV, am, ap, bm, bp))

    gather = [{} for _ in streams]
    for h in range(2):
        for p in range(4 * h, 4 * h + 4):
            if p:
                arrive[p].wait_recv()
        first = row(HERE, h, HERE)
        rows = slice(h * 64, h * 64 + 64)
        for g in range(3):
            cols = slice(g * TAIL, (g + 1) * TAIL)
            xs[first : first + HALF, cols] = jnp.dot(
                squeeze, land[rows, cols], preferred_element_type=F32
            ).astype(BF16)
        tail = jnp.zeros((HALF, TAIL), F32)
        for g in range(3):
            cols = slice(g * TAIL, (g + 1) * TAIL)
            tail += jnp.dot(squeeze_tail[g], land[rows, cols], preferred_element_type=F32)
        xs[first : first + HALF, MAIN:D] = tail.astype(BF16)
        xs[first : first + HALF, D:] = jnp.dot(
            squeeze, land[rows, MAIN:], preferred_element_type=F32
        ).astype(BF16)
        for i in (2 * h, 2 * h + 1):
            _, cols, _, near, next_, af, ab, bf, bb = streams[i]
            own, got = xb(HERE, h, HERE, cols), gather[i]
            got["a", near] = copies.start(own, xb(HERE, h, near, cols), af)
            got["b", near, HERE] = copies.start(own, xb(near, h, HERE, cols), bf)
        for i in (2 * h, 2 * h + 1):
            _, cols, _, near, next_, af, ab, bf, bb = streams[i]
            own, got = xb(HERE, h, HERE, cols), gather[i]
            got["a", next_] = copies.start(own, xb(HERE, h, next_, cols), ab)
            got["b", next_, HERE] = copies.start(own, xb(next_, h, HERE, cols), bb)

    def sx(dz, c):
        return shx.at[pl.ds((c * 4 + dz) * TOK, TOK)]

    ring = [
        copies.start(sx(HERE, 0), sx(PREV, 0), zp),
        copies.start(sx(HERE, 0), sx(NEXT, 0), zm),
    ]
    to_twin = [copies.start(sx(HERE, 0), sx(HERE, 1), twin)]

    def part(ref, cols):
        return ref.at[:, cols]

    def along_b(i, a):
        h, cols, _, near, next_, af, ab, bf, bb = streams[i]
        gather[i]["b", near, a] = copies.start(xb(HERE, h, a, cols), xb(near, h, a, cols), bf)
        gather[i]["b", next_, a] = copies.start(xb(HERE, h, a, cols), xb(next_, h, a, cols), bb)

    def pass_b(i, a):
        h, cols, _, near, next_, af, ab, bf, bb = streams[i]
        gather[i]["b", near, a].wait_recv()
        gather[i]["b", FAR, a] = copies.start(xb(near, h, a, cols), xb(FAR, h, a, cols), bf)

    four = range(4)
    for i in four:
        h, cols, _, near, next_, af, ab, bf, bb = streams[i]
        gather[i]["a", near].wait_recv()
        gather[i]["a", FAR] = copies.start(xb(HERE, h, near, cols), xb(HERE, h, FAR, cols), af)
        along_b(i, near)
    for i in four:
        pass_b(i, HERE)
    for i in four:
        gather[i]["a", streams[i][4]].wait_recv()
        along_b(i, streams[i][4])
    for i in four:
        gather[i]["a", FAR].wait_recv()
        along_b(i, FAR)

    def routed(start, rows):
        at = pl.ds(start, rows)
        gate = xs[at, D:].astype(F32)
        for k in range(3):
            both = jnp.dot(xs[at, 0:D], wgu[k], preferred_element_type=F32)
            value = jax.nn.silu(both[:, :128]) * both[:, 128:] * gate[:, k : k + 1]
            hid[0:rows, k * 128 : (k + 1) * 128] = value.astype(BF16)

        @pl.loop(0, D // 512)
        def _(n):
            cols = pl.ds(pl.multiple_of(n * 512, 512), 512)
            ys[at, cols] = jnp.dot(
                hid[0:rows, :], wd[:, cols], preferred_element_type=F32
            ).astype(BF16)

    for copy in load_routed:
        copy.wait()
    routed(row(HERE, 0, 0), 8 * HALF)
    for i in four:
        pass_b(i, streams[i][3])
    ring[0].wait_recv()
    ring.append(copies.start(part(sx(PREV, 0), lo), part(sx(FAR, 0), lo), zp))
    to_twin.append(copies.start(sx(PREV, 0), sx(PREV, 1), twin))
    ring[1].wait_recv()
    ring.append(copies.start(part(sx(NEXT, 0), hi), part(sx(FAR, 0), hi), zm))
    to_twin.append(copies.start(sx(NEXT, 0), sx(NEXT, 1), twin))
    for i in four:
        pass_b(i, streams[i][4])
    for i in four:
        pass_b(i, FAR)

    for copy in load_shared:
        copy.wait()

    def shared(c):
        @pl.loop(0, 2)
        def _(i):
            at = pl.ds(pl.multiple_of(c * 4 * TOK + i * 2 * TOK, 2 * TOK), 2 * TOK)
            both = jnp.dot(shx[at, :], sgu[...], preferred_element_type=F32)
            shh[...] = (jax.nn.silu(both[:, :SH]) * both[:, SH:]).astype(BF16)

            @pl.loop(0, D // 512)
            def _(n):
                cols = pl.ds(pl.multiple_of(n * 512, 512), 512)
                shp[at, cols] = lax.dot_general(
                    shh[...], sd[cols, :], (((1,), (1,)), ((), ())), preferred_element_type=F32
                ).astype(BF16)

    ring[2].wait_recv()
    ring[3].wait_recv()
    to_twin.append(copies.start(sx(FAR, 0), sx(FAR, 1), twin))
    for copy in to_twin:
        copy.wait_recv()
    shared(1)
    sums = [
        copies.start(shp.at[pl.ds((4 + dz) * TOK, TOK)], sib.at[pl.ds(dz * TOK, TOK)], twin)
        for dz in range(4)
    ]

    groups = ((1, PREV), (0, HERE))

    def yb(b, h, a, n, cols):
        return ys.at[pl.ds(row(b, h, a), n * HALF), cols]

    def spot(g):
        return pl.ds(2 * g * HALF, 2 * HALF)

    reduce = [{} for _ in streams]

    def direct(i):
        h, _, cols, near, next_, af, ab, bf, bb = streams[i]
        for g, a in groups:
            reduce[i]["behind", g] = copies.start(
                yb(near, h, a, 2, cols), behind.at[h, spot(g), cols], bb
            )

    for b in (PREV, NEXT):
        for i in four:
            if b != streams[i][3]:
                for a in four:
                    gather[i]["b", b, a].wait_recv()
        routed(row(b, 0, 0), 8 * HALF)
        for i in four:
            if streams[i][3] == b:
                direct(i)
    shared(0)
    for h in range(2):
        for i in (2 * h, 2 * h + 1):
            for a in four:
                gather[i]["b", FAR, a].wait_recv()
        routed(row(FAR, h, 0), 4 * HALF)
        for g, a in groups:
            for i in (2 * h, 2 * h + 1):
                _, _, cols, near, next_, af, ab, bf, bb = streams[i]
                reduce[i]["far", g] = copies.start(
                    yb(FAR, h, a, 2, cols), r1.at[h, spot(g), cols], bf
                )

    every = pl.ds(0, D)
    for copy in sums:
        copy.wait_recv()
    add_rows(shp, 0, 4 * TOK, every, [(sib, 0)])

    def sp(dz):
        return shp.at[pl.ds(dz * TOK, TOK)]

    zs = [
        copies.start(part(sp(FAR), lo), part(u1, lo), zp),
        copies.start(part(sp(FAR), hi), part(u1, hi), zm),
    ]

    for g, a in groups:
        for i in four:
            h, _, cols, near, next_, af, ab, bf, bb = streams[i]
            reduce[i]["far", g].wait_recv()
            add_rows(ys, row(next_, h, a), 2 * HALF, cols, [(r1.at[h], 2 * g * HALF)])
            reduce[i]["ahead", g] = copies.start(
                yb(next_, h, a, 2, cols), ahead.at[h, spot(g), cols], bf
            )
    zs[0].wait_recv()
    add_rows(shp, NEXT * TOK, TOK, lo, [(u1, 0)])
    zs.append(copies.start(sp(NEXT), u2.at[0], zp))
    zs[1].wait_recv()
    add_rows(shp, PREV * TOK, TOK, hi, [(u1, 0)])
    zs.append(copies.start(sp(PREV), u2.at[1], zm))

    def pass_a(i):
        h, _, cols, near, next_, af, ab, bf, bb = streams[i]
        reduce[i]["a far"].wait_recv()
        add_rows(ys, row(HERE, h, next_), HALF, cols, [(t1.at[h], 0)])
        reduce[i]["a ahead"] = copies.start(
            yb(HERE, h, next_, 1, cols), tahead.at[h, :, cols], af
        )

    for g, a in groups:
        for i in four:
            h, _, cols, near, next_, af, ab, bf, bb = streams[i]
            reduce[i]["behind", g].wait_recv()
            reduce[i]["ahead", g].wait_recv()
            add_rows(
                ys,
                row(HERE, h, a),
                2 * HALF,
                cols,
                [(ahead.at[h], 2 * g * HALF), (behind.at[h], 2 * g * HALF)],
            )
            if g == 1:
                reduce[i]["a far"] = copies.start(
                    yb(HERE, h, FAR, 1, cols), t1.at[h, :, cols], af
                )
            if near in (a, a + 1):
                reduce[i]["a behind"] = copies.start(
                    yb(HERE, h, near, 1, cols), tbehind.at[h, :, cols], ab
                )
    home = []
    for i in four:
        pass_a(i)
    for h in range(2):
        for i in (2 * h, 2 * h + 1):
            reduce[i]["a behind"].wait_recv()
            reduce[i]["a ahead"].wait_recv()
        first = row(HERE, h, HERE)
        add_rows(ys, first, HALF, every, [(tahead.at[h], 0), (tbehind.at[h], 0)])
        rows = slice(h * 64, h * 64 + 64)
        for g in range(3):
            cols = slice(g * TAIL, (g + 1) * TAIL)
            back[rows, cols] = (
                jnp.dot(spread, ys[first : first + HALF, cols], preferred_element_type=F32)
                + jnp.dot(
                    spread_tail[g], ys[first : first + HALF, MAIN:], preferred_element_type=F32
                )
            ).astype(BF16)
        for p in range(4 * h, 4 * h + 4):
            piece = pl.ds(p * PIECE, PIECE)
            if p:
                home.append(copies.start(back.at[piece], ret.at[piece], ep_from[ORDER[p]]))
            else:
                ret[piece, :] = back[piece, :]

    for copy in zs[2:]:
        copy.wait_recv()
    for copy in home:
        copy.wait_recv()
    over = (((0,), (0,)), ((), ()))
    for n in range(4):
        cols = slice(n * TAIL, (n + 1) * TAIL)
        if n < 3:
            total = lax.dot_general(place, ret[:, cols], over, preferred_element_type=F32)
        else:
            total = jnp.zeros((TOK, TAIL), F32)
            for g in range(3):
                total += lax.dot_general(
                    place_tail[g],
                    ret[:, g * TAIL : (g + 1) * TAIL],
                    over,
                    preferred_element_type=F32,
                )
        total += shp[0:TOK, cols].astype(F32)
        total += u2[0, :, cols].astype(F32) + u2[1, :, cols].astype(F32)
        out_ref[:, cols] = total.astype(BF16)

    for copy in copies.made:
        copy.wait_send()


def local(
    tokens,
    expert_ids,
    devices,
    slots,
    gates,
    w_gate,
    w_up,
    w_down,
    shared_gate,
    shared_up,
    shared_down,
):
    vmem = pl.BlockSpec(memory_space=pltpu.VMEM)
    anywhere = pl.BlockSpec(memory_space=pl.ANY)
    copies = 7 + 60 + 4 + 4 + 36 + 4 + 4 + 7
    return pl.pallas_call(
        kernel,
        out_shape=jax.ShapeDtypeStruct((TOK, D), BF16),
        in_specs=[vmem] * 4 + [anywhere] * 7,
        out_specs=vmem,
        scratch_shapes=[
            pltpu.VMEM((3, D, 256), BF16),
            pltpu.VMEM((384, D), BF16),
            pltpu.VMEM((D, 2 * SH), BF16),
            pltpu.VMEM((D, SH), BF16),
            pltpu.VMEM((TOK, MAIN + 128), BF16),
            pltpu.VMEM((TOK, MAIN + 128), BF16),
            pltpu.VMEM((32 * HALF, WIDE), BF16),
            pltpu.VMEM((32 * HALF, D), BF16),
            pltpu.VMEM((8 * HALF, 384), BF16),
            pltpu.VMEM((2, 4 * HALF, D), BF16),
            pltpu.VMEM((2, 4 * HALF, D), BF16),
            pltpu.VMEM((2, 4 * HALF, D), BF16),
            pltpu.VMEM((2, HALF, D), BF16),
            pltpu.VMEM((2, HALF, D), BF16),
            pltpu.VMEM((2, HALF, D), BF16),
            pltpu.VMEM((TOK, MAIN), BF16),
            pltpu.VMEM((TOK, MAIN), BF16),
            pltpu.VMEM((8 * TOK, D), BF16),
            pltpu.VMEM((8 * TOK, D), BF16),
            pltpu.VMEM((2 * TOK, SH), BF16),
            pltpu.VMEM((4 * TOK, D), BF16),
            pltpu.VMEM((TOK, D), BF16),
            pltpu.VMEM((2, TOK, D), BF16),
            pltpu.SemaphoreType.DMA((copies,)),
            pltpu.SemaphoreType.DMA((copies,)),
            pltpu.SemaphoreType.DMA((16,)),
        ],
        compiler_params=pltpu.CompilerParams(
            collective_id=0, has_side_effects=True, vmem_limit_bytes=62 * 1024 * 1024
        ),
        cost_estimate=pl.CostEstimate(
            flops=13_100_000_000, bytes_accessed=12_000_000, transcendentals=900_000
        ),
    )(
        expert_ids.T,
        devices.T,
        slots.T,
        gates.T,
        tokens,
        w_gate,
        w_up,
        w_down,
        shared_gate,
        shared_up,
        shared_down,
    )


def solution(mesh):
    in_specs = (
        P(("seq", "ep"), None),
        P(("seq", "ep"), None),
        P(("seq", "ep"), None),
        P(("seq", "ep"), None),
        P(("seq", "ep"), None),
        P("ep", None, "seq"),
        P("ep", None, "seq"),
        P("ep", "seq", None),
        P(None, "ep"),
        P(None, "ep"),
        P(None, "ep"),
    )
    out_specs = P(("seq", "ep"), None)
    return jax.shard_map(local, mesh=mesh, in_specs=in_specs, out_specs=out_specs, check_vma=False)
```

time: 126 us -> 117 us (0.929)
  the two profiles are of different devices: /device:TPU:36 before, /device:TPU:1 now
where the time goes in v2:
time: 117 us
  Pallas kernels  115 us (98%)
  local copies, waits for them, and re-layouts  1.97 us (2%)
    pallas_call x1, Pallas kernels, local(): pl.pallas_call(kernel, out_shape=jax.ShapeDtypeStruct((TOK, D), BF16), in...  115 us

profile of v2, /device:TPU:1, one launch (start us, length us, event | category | flops | bytes accessed | tf_op | source)
XLA Modules:
  0.0 117.1 jit_solution(1697911360996725649)
XLA Ops:
  0.0 115.1 %shard_map.109 = bf16[128,2560]{1,0:T(8,128)(2,1)} custom-call(s32[6,128]{1,0:T(8,128)} %bitcast.4, s32[3,128]{1,0:T(4,128)} %bitcast.6, s32[3,128]{1,0:T(4,128)} %bitcast.7, f32[6,128]{1,0:T(8,128)} %bitcast.5, bf16[128,2560]{1,0:T(8,128)(2,1)} %tok_hbm.1, bf16[3,2560,128]{2,1,0:T(8,128)(2,1)} %wg_hbm.1, bf16[3,2560,128]{2,1,0:T(8,128)(2,1)} %wu_hbm.1, ...), custom_call_target="tpu_custom_call" | custom-call | flops 13100000256 | bytes 12000000 | tf_op jit(solution)/shard_map/pallas_call | solution.py:511
  115.1 2.0 %copy.13 = bf16[128,2560]{1,0:T(8,128)(2,1)} copy(bf16[128,2560]{1,0:T(8,128)(2,1)} %shard_map.109) | data formatting | bytes 1310720

commit v3 on v2

--- a/solution.py
+++ b/solution.py
@@ -15,7 +15,6 @@
 N_EP = 8
 TOK = 128
 D = 2560
-WIDE = D + 128
 CAP = 12
 PIECE = 16
 HALF = 4 * CAP
@@ -48,17 +47,20 @@
 
 
 def add_rows(dst, start, rows, cols, terms):
-    @pl.loop(0, rows // 16)
+    step = 48 if rows % 48 == 0 else 32
+
+    @pl.loop(0, rows // step)
     def _(i):
-        at = pl.ds(pl.multiple_of(start + i * 16, 16), 16)
+        at = pl.ds(pl.multiple_of(start + i * step, 16), step)
         total = dst[at, cols].astype(F32)
         for ref, first in terms:
-            total += ref[pl.ds(pl.multiple_of(first + i * 16, 16), 16), cols].astype(F32)
+            total += ref[pl.ds(pl.multiple_of(first + i * step, 16), step), cols].astype(F32)
         dst[at, cols] = total.astype(BF16)
 
 
 def row(b, h, a):
-    return ((b * 2 + h) * 4 + a) * HALF
+    pair = a // 2
+    return (((pair * 4 + (b + pair) % 4) * 2 + h) * 2 + a % 2) * HALF
 
 
 def kernel(
@@ -80,6 +82,8 @@
     sd,
     send,
     land,
+    gates_all,
+    gate_cols,
     xs,
     ys,
     hid,
@@ -115,9 +119,10 @@
     ep_to = [(seq, lax.rem(ep + r, N_EP)) for r in range(N_EP)]
     ep_from = [(seq, lax.rem(ep + N_EP - r, N_EP)) for r in range(N_EP)]
     rings = [((xp, xm), (yp, ym)), ((yp, ym), (xp, xm))]
+    xf, yf = (y * SIDE + up(x, 2), ep), (up(y, 2) * SIDE + x, ep)
 
     barrier = pltpu.get_barrier_semaphore()
-    partners = [xp, xm, yp, ym] + ep_to[1:]
+    partners = [xp, xm, xf, yp, ym, yf] + ep_to[1:]
     for device in partners:
         pl.semaphore_signal(barrier, inc=1, device_id=device, device_id_type=MESH)
 
@@ -185,11 +190,15 @@
     pl.semaphore_wait(barrier, len(partners))
     copies = Copies(send_sem, recv_sem)
 
+    def sx(dz, c):
+        return shx.at[pl.ds((dz * 2 + c) * TOK, TOK)]
+
     arrive = [None]
     for p in range(1, N_EP):
         piece = pl.ds(p * PIECE, PIECE)
         arrive.append(copies.start(send.at[piece], land.at[piece], ep_to[ORDER[p]]))
     land[0:PIECE, :] = send[0:PIECE, :]
+    to_twin = [copies.start(sx(HERE, 0), sx(HERE, 1), twin)]
 
     def dense(flip, g=None):
         shape = (4 * PIECE, HALF) if flip else (HALF, 4 * PIECE)
@@ -208,7 +217,6 @@
     spread, spread_tail = dense(True), [dense(True, g) for g in range(3)]
 
     lo, hi = pl.ds(0, LEFT), pl.ds(LEFT, D - LEFT)
-    wide_hi = pl.ds(LEFT, WIDE - LEFT)
 
     def xb(b, h, a, cols):
         return xs.at[pl.ds(row(b, h, a), HALF), cols]
@@ -216,8 +224,8 @@
     streams = []
     for h in range(2):
         (ap, am), (bp, bm) = rings[h]
-        streams.append((h, lo, lo, PREV, NEXT, ap, am, bp, bm))
-        streams.append((h, wide_hi, hi, NEXT, PREV, am, ap, bm, bp))
+        streams.append((h, lo, PREV, NEXT, ap, am, bp, bm))
+        streams.append((h, hi, NEXT, PREV, am, ap, bm, bp))
 
     gather = [{} for _ in streams]
     for h in range(2):
@@ -236,75 +244,130 @@
             cols = slice(g * TAIL, (g + 1) * TAIL)
             tail += jnp.dot(squeeze_tail[g], land[rows, cols], preferred_element_type=F32)
         xs[first : first + HALF, MAIN:D] = tail.astype(BF16)
-        xs[first : first + HALF, D:] = jnp.dot(
-            squeeze, land[rows, MAIN:], preferred_element_type=F32
-        ).astype(BF16)
         for i in (2 * h, 2 * h + 1):
-            _, cols, _, near, next_, af, ab, bf, bb = streams[i]
+            _, cols, near, next_, af, ab, bf, bb = streams[i]
             own, got = xb(HERE, h, HERE, cols), gather[i]
             got["a", near] = copies.start(own, xb(HERE, h, near, cols), af)
             got["b", near, HERE] = copies.start(own, xb(near, h, HERE, cols), bf)
         for i in (2 * h, 2 * h + 1):
-            _, cols, _, near, next_, af, ab, bf, bb = streams[i]
+            _, cols, near, next_, af, ab, bf, bb = streams[i]
             own, got = xb(HERE, h, HERE, cols), gather[i]
             got["a", next_] = copies.start(own, xb(HERE, h, next_, cols), ab)
             got["b", next_, HERE] = copies.start(own, xb(next_, h, HERE, cols), bb)
 
-    def sx(dz, c):
-        return shx.at[pl.ds((c * 4 + dz) * TOK, TOK)]
+    lands = lax.broadcasted_iota(jnp.int32, (TOK, TOK), 0)
+    slots_i = lax.broadcasted_iota(jnp.int32, (TOK, TOK), 1)
+    which = jnp.zeros((TOK, TOK), F32)
+    for p in range(N_EP):
+        inside = (slots_i >= CAP * p) & (slots_i < CAP * (p + 1))
+        which = jnp.where(inside & (lands == slots_i + (PIECE - CAP) * p), 1.0, which)
+    turned = lax.dot_general(
+        land[:, MAIN:],
+        which.astype(BF16),
+        (((0,), (0,)), ((), ())),
+        preferred_element_type=F32,
+    )
+    gates_all[0:16, :] = turned[0:16, :].astype(BF16)
+
+    def tiles(ry, rx, n):
+        return gates_all.at[pl.ds((ry * 4 + rx) * 16, n * 16)]
+
+    gate_copies = [
+        copies.start(tiles(HERE, HERE, 1), tiles(HERE, PREV, 1), xp),
+        copies.start(tiles(HERE, HERE, 1), tiles(HERE, NEXT, 1), xm),
+        copies.start(tiles(HERE, HERE, 1), tiles(HERE, FAR, 1), xf),
+    ]
 
     ring = [
         copies.start(sx(HERE, 0), sx(PREV, 0), zp),
         copies.start(sx(HERE, 0), sx(NEXT, 0), zm),
     ]
-    to_twin = [copies.start(sx(HERE, 0), sx(HERE, 1), twin)]
 
     def part(ref, cols):
         return ref.at[:, cols]
 
     def along_b(i, a):
-        h, cols, _, near, next_, af, ab, bf, bb = streams[i]
+        h, cols, near, next_, af, ab, bf, bb = streams[i]
         gather[i]["b", near, a] = copies.start(xb(HERE, h, a, cols), xb(near, h, a, cols), bf)
         gather[i]["b", next_, a] = copies.start(xb(HERE, h, a, cols), xb(next_, h, a, cols), bb)
 
     def pass_b(i, a):
-        h, cols, _, near, next_, af, ab, bf, bb = streams[i]
+        h, cols, near, next_, af, ab, bf, bb = streams[i]
         gather[i]["b", near, a].wait_recv()
         gather[i]["b", FAR, a] = copies.start(xb(near, h, a, cols), xb(FAR, h, a, cols), bf)
 
+    sums = {}
+
+    def shared(dz):
+        at = pl.ds(dz * 2 * TOK, 2 * TOK)
+        both = jnp.dot(shx[at, :], sgu[...], preferred_element_type=F32)
+        shh[...] = (jax.nn.silu(both[:, :SH]) * both[:, SH:]).astype(BF16)
+
+        @pl.loop(0, D // 512)
+        def _(n):
+            cols = pl.ds(pl.multiple_of(n * 512, 512), 512)
+            shp[at, cols] = lax.dot_general(
+                shh[...], sd[cols, :], (((1,), (1,)), ((), ())), preferred_element_type=F32
+            ).astype(BF16)
+
+        sums[dz] = copies.start(
+            shp.at[pl.ds((dz * 2 + 1) * TOK, TOK)], sib.at[pl.ds(dz * TOK, TOK)], twin
+        )
+
+    for copy in load_shared:
+        copy.wait()
+    to_twin[0].wait_recv()
+    shared(HERE)
+
     four = range(4)
     for i in four:
-        h, cols, _, near, next_, af, ab, bf, bb = streams[i]
+        h, cols, near, next_, af, ab, bf, bb = streams[i]
         gather[i]["a", near].wait_recv()
         gather[i]["a", FAR] = copies.start(xb(HERE, h, near, cols), xb(HERE, h, FAR, cols), af)
         along_b(i, near)
     for i in four:
         pass_b(i, HERE)
     for i in four:
-        gather[i]["a", streams[i][4]].wait_recv()
-        along_b(i, streams[i][4])
+        gather[i]["a", streams[i][3]].wait_recv()
+        along_b(i, streams[i][3])
+    for copy in gate_copies[:3]:
+        copy.wait_recv()
+    gate_copies += [
+        copies.start(tiles(HERE, HERE, 4), tiles(PREV, HERE, 4), yp),
+        copies.start(tiles(HERE, HERE, 4), tiles(NEXT, HERE, 4), ym),
+        copies.start(tiles(HERE, HERE, 4), tiles(FAR, HERE, 4), yf),
+    ]
     for i in four:
         gather[i]["a", FAR].wait_recv()
         along_b(i, FAR)
 
+    def experts(start, rows):
+        spots = {row(b, h, a): (h, a, b) for b in four for h in range(2) for a in four}
+        columns = []
+        for first in range(start, start + rows, HALF):
+            h, a, b = spots[first]
+            columns.append((h, (b * 4 + a if h == 0 else a * 4 + b) * 16))
+        at = pl.ds(start, rows)
+        for k in range(3):
+            both = jnp.dot(xs[at, :], wgu[k], preferred_element_type=F32)
+            gate = jnp.concatenate([gate_cols[h, :, c + k : c + k + 1] for h, c in columns], 0)
+            value = jax.nn.silu(both[:, :128]) * both[:, 128:] * gate
+            hid[0:rows, k * 128 : (k + 1) * 128] = value.astype(BF16)
+
+    def down(start, rows, cols):
+        ys[pl.ds(start, rows), cols] = jnp.dot(
+            hid[0:rows, :], wd[:, cols], preferred_element_type=F32
+        ).astype(BF16)
+
     def routed(start, rows):
-        at = pl.ds(start, rows)
-        gate = xs[at, D:].astype(F32)
-        for k in range(3):
-            both = jnp.dot(xs[at, 0:D], wgu[k], preferred_element_type=F32)
-            value = jax.nn.silu(both[:, :128]) * both[:, 128:] * gate[:, k : k + 1]
-            hid[0:rows, k * 128 : (k + 1) * 128] = value.astype(BF16)
+        experts(start, rows)
 
         @pl.loop(0, D // 512)
         def _(n):
-            cols = pl.ds(pl.multiple_of(n * 512, 512), 512)
-            ys[at, cols] = jnp.dot(
-                hid[0:rows, :], wd[:, cols], preferred_element_type=F32
-            ).astype(BF16)
-
-    for copy in load_routed:
-        copy.wait()
-    routed(row(HERE, 0, 0), 8 * HALF)
+            down(start, rows, pl.ds(pl.multiple_of(n * 512, 512), 512))
+
+    for i in four:
+        pass_b(i, streams[i][2])
     for i in four:
         pass_b(i, streams[i][3])
     ring[0].wait_recv()
@@ -313,40 +376,36 @@
     ring[1].wait_recv()
     ring.append(copies.start(part(sx(NEXT, 0), hi), part(sx(FAR, 0), hi), zm))
     to_twin.append(copies.start(sx(NEXT, 0), sx(NEXT, 1), twin))
-    for i in four:
-        pass_b(i, streams[i][4])
+    for copy in load_routed:
+        copy.wait()
+    for copy in gate_copies[3:]:
+        copy.wait_recv()
+    for h in range(2):
+        spots = lax.broadcasted_iota(jnp.int32, (HALF, TOK), 1) == (
+            lax.broadcasted_iota(jnp.int32, (HALF, TOK), 0) + h * HALF
+        )
+        gate_cols[h] = lax.dot_general(
+            jnp.where(spots, 1.0, 0.0).astype(BF16),
+            gates_all[...],
+            (((1,), (1,)), ((), ())),
+            preferred_element_type=F32,
+        )
+    for a in (HERE, NEXT):
+        for i in four:
+            gather[i]["b", streams[i][3], a].wait_recv()
+    routed(0, 12 * HALF)
+    to_twin[1].wait_recv()
+    to_twin[2].wait_recv()
+    shared(PREV)
+    shared(NEXT)
     for i in four:
         pass_b(i, FAR)
-
-    for copy in load_shared:
-        copy.wait()
-
-    def shared(c):
-        @pl.loop(0, 2)
-        def _(i):
-            at = pl.ds(pl.multiple_of(c * 4 * TOK + i * 2 * TOK, 2 * TOK), 2 * TOK)
-            both = jnp.dot(shx[at, :], sgu[...], preferred_element_type=F32)
-            shh[...] = (jax.nn.silu(both[:, :SH]) * both[:, SH:]).astype(BF16)
-
-            @pl.loop(0, D // 512)
-            def _(n):
-                cols = pl.ds(pl.multiple_of(n * 512, 512), 512)
-                shp[at, cols] = lax.dot_general(
-                    shh[...], sd[cols, :], (((1,), (1,)), ((), ())), preferred_element_type=F32
-                ).astype(BF16)
-
     ring[2].wait_recv()
     ring[3].wait_recv()
     to_twin.append(copies.start(sx(FAR, 0), sx(FAR, 1), twin))
-    for copy in to_twin:
-        copy.wait_recv()
-    shared(1)
-    sums = [
-        copies.start(shp.at[pl.ds((4 + dz) * TOK, TOK)], sib.at[pl.ds(dz * TOK, TOK)], twin)
-        for dz in range(4)
-    ]
 
     groups = ((1, PREV), (0, HERE))
+    phases = ((pl.ds(0, TAIL), pl.ds(MAIN, TAIL)), (pl.ds(TAIL, TAIL), pl.ds(2 * TAIL, TAIL)))
 
     def yb(b, h, a, n, cols):
         return ys.at[pl.ds(row(b, h, a), n * HALF), cols]
@@ -356,115 +415,135 @@
 
     reduce = [{} for _ in streams]
 
-    def direct(i):
-        h, _, cols, near, next_, af, ab, bf, bb = streams[i]
-        for g, a in groups:
+    def direct(g, a):
+        for i in four:
+            h, cols, near, next_, af, ab, bf, bb = streams[i]
             reduce[i]["behind", g] = copies.start(
                 yb(near, h, a, 2, cols), behind.at[h, spot(g), cols], bb
             )
 
-    for b in (PREV, NEXT):
+    direct(0, HERE)
+    for a in (PREV, FAR):
         for i in four:
-            if b != streams[i][3]:
-                for a in four:
-                    gather[i]["b", b, a].wait_recv()
-        routed(row(b, 0, 0), 8 * HALF)
-        for i in four:
-            if streams[i][3] == b:
-                direct(i)
-    shared(0)
-    for h in range(2):
-        for i in (2 * h, 2 * h + 1):
-            for a in four:
-                gather[i]["b", FAR, a].wait_recv()
-        routed(row(FAR, h, 0), 4 * HALF)
+            gather[i]["b", streams[i][3], a].wait_recv()
+    routed(20 * HALF, 12 * HALF)
+    direct(1, PREV)
+    to_twin[3].wait_recv()
+    shared(FAR)
+    for i in four:
+        for a in four:
+            gather[i]["b", FAR, a].wait_recv()
+    experts(12 * HALF, 8 * HALF)
+    for q in range(2):
+        for cols in phases[q]:
+            down(12 * HALF, 8 * HALF, cols)
         for g, a in groups:
-            for i in (2 * h, 2 * h + 1):
-                _, _, cols, near, next_, af, ab, bf, bb = streams[i]
-                reduce[i]["far", g] = copies.start(
+            for i in four:
+                h, _, near, next_, af, ab, bf, bb = streams[i]
+                cols = phases[q][i % 2]
+                reduce[i]["far", q, g] = copies.start(
                     yb(FAR, h, a, 2, cols), r1.at[h, spot(g), cols], bf
                 )
 
+    def sp(dz):
+        return shp.at[pl.ds(dz * 2 * TOK, TOK)]
+
     every = pl.ds(0, D)
-    for copy in sums:
-        copy.wait_recv()
-    add_rows(shp, 0, 4 * TOK, every, [(sib, 0)])
-
-    def sp(dz):
-        return shp.at[pl.ds(dz * TOK, TOK)]
-
-    zs = [
-        copies.start(part(sp(FAR), lo), part(u1, lo), zp),
-        copies.start(part(sp(FAR), hi), part(u1, hi), zm),
-    ]
-
-    for g, a in groups:
-        for i in four:
-            h, _, cols, near, next_, af, ab, bf, bb = streams[i]
-            reduce[i]["far", g].wait_recv()
-            add_rows(ys, row(next_, h, a), 2 * HALF, cols, [(r1.at[h], 2 * g * HALF)])
-            reduce[i]["ahead", g] = copies.start(
-                yb(next_, h, a, 2, cols), ahead.at[h, spot(g), cols], bf
-            )
+    for dz in (FAR, NEXT, PREV, HERE):
+        sums[dz].wait_recv()
+        add_rows(shp, dz * 2 * TOK, TOK, every, [(sib, dz * TOK)])
+        if dz == FAR:
+            zs = [
+                copies.start(part(sp(FAR), lo), part(u1, lo), zp),
+                copies.start(part(sp(FAR), hi), part(u1, hi), zm),
+            ]
+
+    for q in range(2):
+        for g, a in groups:
+            for i in four:
+                h, _, near, next_, af, ab, bf, bb = streams[i]
+                cols = phases[q][i % 2]
+                reduce[i]["far", q, g].wait_recv()
+                add_rows(ys, row(next_, h, a), 2 * HALF, cols, [(r1.at[h], 2 * g * HALF)])
+                reduce[i]["ahead", q, g] = copies.start(
+                    yb(next_, h, a, 2, cols), ahead.at[h, spot(g), cols], bf
+                )
     zs[0].wait_recv()
-    add_rows(shp, NEXT * TOK, TOK, lo, [(u1, 0)])
+    add_rows(shp, NEXT * 2 * TOK, TOK, lo, [(u1, 0)])
     zs.append(copies.start(sp(NEXT), u2.at[0], zp))
     zs[1].wait_recv()
-    add_rows(shp, PREV * TOK, TOK, hi, [(u1, 0)])
+    add_rows(shp, PREV * 2 * TOK, TOK, hi, [(u1, 0)])
     zs.append(copies.start(sp(PREV), u2.at[1], zm))
 
-    def pass_a(i):
-        h, _, cols, near, next_, af, ab, bf, bb = streams[i]
-        reduce[i]["a far"].wait_recv()
-        add_rows(ys, row(HERE, h, next_), HALF, cols, [(t1.at[h], 0)])
-        reduce[i]["a ahead"] = copies.start(
-            yb(HERE, h, next_, 1, cols), tahead.at[h, :, cols], af
-        )
-
-    for g, a in groups:
+    def end_b(q):
+        for g, a in groups:
+            for i in four:
+                h, _, near, next_, af, ab, bf, bb = streams[i]
+                cols = phases[q][i % 2]
+                if q == 0:
+                    reduce[i]["behind", g].wait_recv()
+                reduce[i]["ahead", q, g].wait_recv()
+                add_rows(
+                    ys,
+                    row(HERE, h, a),
+                    2 * HALF,
+                    cols,
+                    [(ahead.at[h], 2 * g * HALF), (behind.at[h], 2 * g * HALF)],
+                )
+                if g == 1:
+                    reduce[i]["a far", q] = copies.start(
+                        yb(HERE, h, FAR, 1, cols), t1.at[h, :, cols], af
+                    )
+                if near in (a, a + 1):
+                    reduce[i]["a behind", q] = copies.start(
+                        yb(HERE, h, near, 1, cols), tbehind.at[h, :, cols], ab
+                    )
+
+    def pass_a(q):
         for i in four:
-            h, _, cols, near, next_, af, ab, bf, bb = streams[i]
-            reduce[i]["behind", g].wait_recv()
-            reduce[i]["ahead", g].wait_recv()
-            add_rows(
-                ys,
-                row(HERE, h, a),
-                2 * HALF,
-                cols,
-                [(ahead.at[h], 2 * g * HALF), (behind.at[h], 2 * g * HALF)],
+            h, _, near, next_, af, ab, bf, bb = streams[i]
+            cols = phases[q][i % 2]
+            reduce[i]["a far", q].wait_recv()
+            add_rows(ys, row(HERE, h, next_), HALF, cols, [(t1.at[h], 0)])
+            reduce[i]["a ahead", q] = copies.start(
+                yb(HERE, h, next_, 1, cols), tahead.at[h, :, cols], af
             )
-            if g == 1:
-                reduce[i]["a far"] = copies.start(
-                    yb(HERE, h, FAR, 1, cols), t1.at[h, :, cols], af
-                )
-            if near in (a, a + 1):
-                reduce[i]["a behind"] = copies.start(
-                    yb(HERE, h, near, 1, cols), tbehind.at[h, :, cols], ab
-                )
+
     home = []
-    for i in four:
-        pass_a(i)
-    for h in range(2):
-        for i in (2 * h, 2 * h + 1):
-            reduce[i]["a behind"].wait_recv()
-            reduce[i]["a ahead"].wait_recv()
-        first = row(HERE, h, HERE)
-        add_rows(ys, first, HALF, every, [(tahead.at[h], 0), (tbehind.at[h], 0)])
-        rows = slice(h * 64, h * 64 + 64)
-        for g in range(3):
-            cols = slice(g * TAIL, (g + 1) * TAIL)
-            back[rows, cols] = (
-                jnp.dot(spread, ys[first : first + HALF, cols], preferred_element_type=F32)
-                + jnp.dot(
-                    spread_tail[g], ys[first : first + HALF, MAIN:], preferred_element_type=F32
-                )
-            ).astype(BF16)
-        for p in range(4 * h, 4 * h + 4):
-            piece = pl.ds(p * PIECE, PIECE)
-            if p:
-                home.append(copies.start(back.at[piece], ret.at[piece], ep_from[ORDER[p]]))
-            else:
-                ret[piece, :] = back[piece, :]
+
+    def end_a(q):
+        for h in range(2):
+            first = row(HERE, h, HERE)
+            for i in (2 * h, 2 * h + 1):
+                reduce[i]["a behind", q].wait_recv()
+                reduce[i]["a ahead", q].wait_recv()
+                cols = phases[q][i % 2]
+                add_rows(ys, first, HALF, cols, [(tahead.at[h], 0), (tbehind.at[h], 0)])
+            rows = slice(h * 64, h * 64 + 64)
+            for g in ((0,), (1, 2))[q]:
+                cols = slice(g * TAIL, (g + 1) * TAIL)
+                back[rows, cols] = (
+                    jnp.dot(spread, ys[first : first + HALF, cols], preferred_element_type=F32)
+                    + jnp.dot(
+                        spread_tail[g], ys[first : first + HALF, MAIN:], preferred_element_type=F32
+                    )
+                ).astype(BF16)
+            cols = (pl.ds(0, TAIL), pl.ds(TAIL, 2 * TAIL))[q]
+            for p in range(4 * h, 4 * h + 4):
+                piece = pl.ds(p * PIECE, PIECE)
+                if p:
+                    home.append(
+                        copies.start(back.at[piece, cols], ret.at[piece, cols], ep_from[ORDER[p]])
+                    )
+                else:
+                    ret[piece, cols] = back[piece, cols]
+
+    end_b(0)
+    pass_a(0)
+    end_b(1)
+    end_a(0)
+    pass_a(1)
+    end_a(1)
 
     for copy in zs[2:]:
         copy.wait_recv()
@@ -507,7 +586,7 @@
 ):
     vmem = pl.BlockSpec(memory_space=pltpu.VMEM)
     anywhere = pl.BlockSpec(memory_space=pl.ANY)
-    copies = 7 + 60 + 4 + 4 + 36 + 4 + 4 + 7
+    copies = 7 + 60 + 6 + 4 + 4 + 64 + 4 + 4 + 14
     return pl.pallas_call(
         kernel,
         out_shape=jax.ShapeDtypeStruct((TOK, D), BF16),
@@ -520,9 +599,11 @@
             pltpu.VMEM((D, SH), BF16),
             pltpu.VMEM((TOK, MAIN + 128), BF16),
             pltpu.VMEM((TOK, MAIN + 128), BF16),
-            pltpu.VMEM((32 * HALF, WIDE), BF16),
+            pltpu.VMEM((256, 128), BF16),
+            pltpu.VMEM((2, HALF, 256), F32),
             pltpu.VMEM((32 * HALF, D), BF16),
-            pltpu.VMEM((8 * HALF, 384), BF16),
+            pltpu.VMEM((32 * HALF, D), BF16),
+            pltpu.VMEM((12 * HALF, 384), BF16),
             pltpu.VMEM((2, 4 * HALF, D), BF16),
             pltpu.VMEM((2, 4 * HALF, D), BF16),
             pltpu.VMEM((2, 4 * HALF, D), BF16),

time: 117 us -> 112 us (0.957)
  Pallas kernels: 115 us -> 110 us
    pallas_call x1, Pallas kernels: 115 us -> 110 us  [local(): pl.pallas_call(kernel, out_shape=jax.ShapeDtypeStruct((TOK, D), BF16), in...]
where the time goes in v3:
time: 112 us
  Pallas kernels  110 us (98%)
  local copies, waits for them, and re-layouts  1.97 us (2%)
    pallas_call x1, Pallas kernels, local(): pl.pallas_call(kernel, out_shape=jax.ShapeDtypeStruct((TOK, D), BF16), in...  110 us

profile of v3, /device:TPU:1, one launch (start us, length us, event | category | flops | bytes accessed | tf_op | source)
XLA Modules:
  0.0 111.9 jit_solution(1684339861116855093)
XLA Ops:
  0.0 110.0 %shard_map.109 = bf16[128,2560]{1,0:T(8,128)(2,1)} custom-call(s32[6,128]{1,0:T(8,128)} %bitcast.4, s32[3,128]{1,0:T(4,128)} %bitcast.6, s32[3,128]{1,0:T(4,128)} %bitcast.7, f32[6,128]{1,0:T(8,128)} %bitcast.5, bf16[128,2560]{1,0:T(8,128)(2,1)} %tok_hbm.1, bf16[3,2560,128]{2,1,0:T(8,128)(2,1)} %wg_hbm.1, bf16[3,2560,128]{2,1,0:T(8,128)(2,1)} %wu_hbm.1, ...), custom_call_target="tpu_custom_call" | custom-call | flops 13100000256 | bytes 12000000 | tf_op jit(solution)/shard_map/pallas_call | solution.py:590
  110.0 2.0 %copy.13 = bf16[128,2560]{1,0:T(8,128)(2,1)} copy(bf16[128,2560]{1,0:T(8,128)(2,1)} %shard_map.109) | data formatting | bytes 1310720

commit v4 on v3

--- a/solution.py
+++ b/solution.py
@@ -22,6 +22,7 @@
 LEFT = 1280
 MAIN = 1920
 TAIL = D - MAIN
+EARLY = 896
 ORDER = (0, 1, 2, 7, 6, 3, 4, 5)
 
 HERE, NEXT, PREV, FAR = 0, 1, 2, 3
@@ -64,10 +65,10 @@
 
 
 def kernel(
-    ids_ref,
-    dev_ref,
-    slot_ref,
-    gates_ref,
+    ids_hbm,
+    dev_hbm,
+    slot_hbm,
+    gates_hbm,
     tok_hbm,
     wg_hbm,
     wu_hbm,
@@ -75,6 +76,11 @@
     sg_hbm,
     su_hbm,
     sd_hbm,
+    out_hbm,
+    ids_ref,
+    dev_ref,
+    slot_ref,
+    gates_ref,
     out_ref,
     wgu,
     wd,
@@ -135,6 +141,12 @@
         return copy
 
     tok = shx.at[pl.ds(0, TOK)]
+    load_small = [
+        load(ids_hbm, ids_ref),
+        load(dev_hbm, dev_ref),
+        load(slot_hbm, slot_ref),
+        load(gates_hbm, gates_ref),
+    ]
     load_tok = load(tok_hbm, tok)
     load_routed = []
     for k in range(3):
@@ -149,6 +161,8 @@
 
     rows_i = lax.broadcasted_iota(jnp.int32, (TOK, TOK), 0)
     lanes_i = lax.broadcasted_iota(jnp.int32, (TOK, TOK), 1)
+    for copy in load_small:
+        copy.wait()
     place = jnp.zeros((TOK, TOK), F32)
     place_tail = [jnp.zeros((TOK, TOK), F32) for _ in range(3)]
     gate_of = [jnp.zeros((TOK, TOK), F32) for _ in range(3)]
@@ -194,9 +208,13 @@
         return shx.at[pl.ds((dz * 2 + c) * TOK, TOK)]
 
     arrive = [None]
-    for p in range(1, N_EP):
-        piece = pl.ds(p * PIECE, PIECE)
-        arrive.append(copies.start(send.at[piece], land.at[piece], ep_to[ORDER[p]]))
+
+    def exchange(first, end):
+        for p in range(first, end):
+            piece = pl.ds(p * PIECE, PIECE)
+            arrive.append(copies.start(send.at[piece], land.at[piece], ep_to[ORDER[p]]))
+
+    exchange(1, 4)
     land[0:PIECE, :] = send[0:PIECE, :]
     to_twin = [copies.start(sx(HERE, 0), sx(HERE, 1), twin)]
 
@@ -214,7 +232,7 @@
         return hit.astype(BF16)
 
     squeeze, squeeze_tail = dense(False), [dense(False, g) for g in range(3)]
-    spread, spread_tail = dense(True), [dense(True, g) for g in range(3)]
+    spread = dense(True)
 
     lo, hi = pl.ds(0, LEFT), pl.ds(LEFT, D - LEFT)
 
@@ -232,6 +250,8 @@
         for p in range(4 * h, 4 * h + 4):
             if p:
                 arrive[p].wait_recv()
+        if h == 0:
+            exchange(4, 8)
         first = row(HERE, h, HERE)
         rows = slice(h * 64, h * 64 + 64)
         for g in range(3):
@@ -405,7 +425,10 @@
     to_twin.append(copies.start(sx(FAR, 0), sx(FAR, 1), twin))
 
     groups = ((1, PREV), (0, HERE))
-    phases = ((pl.ds(0, TAIL), pl.ds(MAIN, TAIL)), (pl.ds(TAIL, TAIL), pl.ds(2 * TAIL, TAIL)))
+    phases = (
+        (pl.ds(0, EARLY), pl.ds(LEFT, EARLY)),
+        (pl.ds(EARLY, LEFT - EARLY), pl.ds(LEFT + EARLY, LEFT - EARLY)),
+    )
 
     def yb(b, h, a, n, cols):
         return ys.at[pl.ds(row(b, h, a), n * HALF), cols]
@@ -492,7 +515,13 @@
                 )
                 if g == 1:
                     reduce[i]["a far", q] = copies.start(
-                        yb(HERE, h, FAR, 1, cols), t1.at[h, :, cols], af
+                        yb(HERE, h, FAR, 1, cols),
+                        t1.at[h, :, cols],
+                        af if q == 0 else (xf, yf)[h],
+                    )
+                if q == 1 and next_ in (a, a + 1):
+                    reduce[i]["a ahead", q] = copies.start(
+                        yb(HERE, h, next_, 1, cols), tahead.at[h, :, cols], af
                     )
                 if near in (a, a + 1):
                     reduce[i]["a behind", q] = copies.start(
@@ -509,66 +538,66 @@
                 yb(HERE, h, next_, 1, cols), tahead.at[h, :, cols], af
             )
 
-    home = []
+    home = [[], []]
+    spans = (slice(0, 2 * EARLY), slice(2 * EARLY, D))
 
     def end_a(q):
         for h in range(2):
             first = row(HERE, h, HERE)
+            rows = slice(h * 64, h * 64 + 64)
             for i in (2 * h, 2 * h + 1):
                 reduce[i]["a behind", q].wait_recv()
                 reduce[i]["a ahead", q].wait_recv()
+                terms = [(tahead.at[h], 0), (tbehind.at[h], 0)]
+                if q == 1:
+                    reduce[i]["a far", q].wait_recv()
+                    terms.append((t1.at[h], 0))
                 cols = phases[q][i % 2]
-                add_rows(ys, first, HALF, cols, [(tahead.at[h], 0), (tbehind.at[h], 0)])
-            rows = slice(h * 64, h * 64 + 64)
-            for g in ((0,), (1, 2))[q]:
-                cols = slice(g * TAIL, (g + 1) * TAIL)
-                back[rows, cols] = (
-                    jnp.dot(spread, ys[first : first + HALF, cols], preferred_element_type=F32)
-                    + jnp.dot(
-                        spread_tail[g], ys[first : first + HALF, MAIN:], preferred_element_type=F32
-                    )
+                add_rows(ys, first, HALF, cols, terms)
+                at = pl.ds(spans[q].start + i % 2 * cols.size, cols.size)
+                back[rows, at] = jnp.dot(
+                    spread, ys[first : first + HALF, cols], preferred_element_type=F32
                 ).astype(BF16)
-            cols = (pl.ds(0, TAIL), pl.ds(TAIL, 2 * TAIL))[q]
+            cols = pl.ds(spans[q].start, spans[q].stop - spans[q].start)
             for p in range(4 * h, 4 * h + 4):
                 piece = pl.ds(p * PIECE, PIECE)
                 if p:
-                    home.append(
+                    home[q].append(
                         copies.start(back.at[piece, cols], ret.at[piece, cols], ep_from[ORDER[p]])
                     )
                 else:
                     ret[piece, cols] = back[piece, cols]
 
+    stores = []
+
+    def finish(q):
+        for copy in home[q]:
+            copy.wait_recv()
+        for i in range(2):
+            cols = phases[q][i]
+            at = pl.ds(spans[q].start + i * cols.size, cols.size)
+            total = lax.dot_general(
+                place, ret[:, at], (((0,), (0,)), ((), ())), preferred_element_type=F32
+            )
+            total += shp[0:TOK, cols].astype(F32)
+            total += u2[0, :, cols].astype(F32) + u2[1, :, cols].astype(F32)
+            out_ref[:, cols] = total.astype(BF16)
+            stores.append(load(out_ref.at[:, cols], out_hbm.at[:, cols]))
+
     end_b(0)
     pass_a(0)
     end_b(1)
     end_a(0)
-    pass_a(1)
     end_a(1)
-
     for copy in zs[2:]:
         copy.wait_recv()
-    for copy in home:
-        copy.wait_recv()
-    over = (((0,), (0,)), ((), ()))
-    for n in range(4):
-        cols = slice(n * TAIL, (n + 1) * TAIL)
-        if n < 3:
-            total = lax.dot_general(place, ret[:, cols], over, preferred_element_type=F32)
-        else:
-            total = jnp.zeros((TOK, TAIL), F32)
-            for g in range(3):
-                total += lax.dot_general(
-                    place_tail[g],
-                    ret[:, g * TAIL : (g + 1) * TAIL],
-                    over,
-                    preferred_element_type=F32,
-                )
-        total += shp[0:TOK, cols].astype(F32)
-        total += u2[0, :, cols].astype(F32) + u2[1, :, cols].astype(F32)
-        out_ref[:, cols] = total.astype(BF16)
+    finish(0)
+    finish(1)
 
     for copy in copies.made:
         copy.wait_send()
+    for copy in stores:
+        copy.wait()
 
 
 def local(
@@ -584,15 +613,19 @@
     shared_up,
     shared_down,
 ):
-    vmem = pl.BlockSpec(memory_space=pltpu.VMEM)
     anywhere = pl.BlockSpec(memory_space=pl.ANY)
     copies = 7 + 60 + 6 + 4 + 4 + 64 + 4 + 4 + 14
     return pl.pallas_call(
         kernel,
         out_shape=jax.ShapeDtypeStruct((TOK, D), BF16),
-        in_specs=[vmem] * 4 + [anywhere] * 7,
-        out_specs=vmem,
+        in_specs=[anywhere] * 11,
+        out_specs=anywhere,
         scratch_shapes=[
+            pltpu.VMEM((6, TOK), jnp.int32),
+            pltpu.VMEM((3, TOK), jnp.int32),
+            pltpu.VMEM((3, TOK), jnp.int32),
+            pltpu.VMEM((6, TOK), F32),
+            pltpu.VMEM((TOK, D), BF16),
             pltpu.VMEM((3, D, 256), BF16),
             pltpu.VMEM((384, D), BF16),
             pltpu.VMEM((D, 2 * SH), BF16),
@@ -610,8 +643,8 @@
             pltpu.VMEM((2, HALF, D), BF16),
             pltpu.VMEM((2, HALF, D), BF16),
             pltpu.VMEM((2, HALF, D), BF16),
-            pltpu.VMEM((TOK, MAIN), BF16),
-            pltpu.VMEM((TOK, MAIN), BF16),
+            pltpu.VMEM((TOK, D), BF16),
+            pltpu.VMEM((TOK, D), BF16),
             pltpu.VMEM((8 * TOK, D), BF16),
             pltpu.VMEM((8 * TOK, D), BF16),
             pltpu.VMEM((2 * TOK, SH), BF16),
@@ -620,7 +653,7 @@
             pltpu.VMEM((2, TOK, D), BF16),
             pltpu.SemaphoreType.DMA((copies,)),
             pltpu.SemaphoreType.DMA((copies,)),
-            pltpu.SemaphoreType.DMA((16,)),
+            pltpu.SemaphoreType.DMA((24,)),
         ],
         compiler_params=pltpu.CompilerParams(
             collective_id=0, has_side_effects=True, vmem_limit_bytes=62 * 1024 * 1024

time: 112 us -> 110 us (0.982)
  Pallas kernels: 110 us -> 108 us
    pallas_call x1, Pallas kernels: 110 us -> 108 us  [local(): pl.pallas_call(kernel, out_shape=jax.ShapeDtypeStruct((TOK, D), BF16), in...]
where the time goes in v4:
time: 110 us
  Pallas kernels  108 us (98%)
  local copies, waits for them, and re-layouts  1.97 us (2%)
    pallas_call x1, Pallas kernels, local(): pl.pallas_call(kernel, out_shape=jax.ShapeDtypeStruct((TOK, D), BF16), in...  108 us

profile of v4, /device:TPU:1, one launch (start us, length us, event | category | flops | bytes accessed | tf_op | source)
XLA Modules:
  0.0 109.8 jit_solution(10782350122037457700)
XLA Ops:
  0.0 107.8 %shard_map.109 = bf16[128,2560]{1,0:T(8,128)(2,1)} custom-call(s32[6,128]{1,0:T(8,128)} %bitcast.4, s32[3,128]{1,0:T(4,128)} %bitcast.6, s32[3,128]{1,0:T(4,128)} %bitcast.7, f32[6,128]{1,0:T(8,128)} %bitcast.5, bf16[128,2560]{1,0:T(8,128)(2,1)} %tok_hbm.1, bf16[3,2560,128]{2,1,0:T(8,128)(2,1)} %wg_hbm.1, bf16[3,2560,128]{2,1,0:T(8,128)(2,1)} %wu_hbm.1, ...), custom_call_target="tpu_custom_call" | custom-call | flops 13100000256 | bytes 12000000 | tf_op jit(solution)/shard_map/pallas_call | solution.py:618
  107.8 2.0 %copy.13 = bf16[128,2560]{1,0:T(8,128)(2,1)} copy(bf16[128,2560]{1,0:T(8,128)(2,1)} %shard_map.109) | data formatting | bytes 1310720

commit v5 on v4

--- a/solution.py
+++ b/solution.py
@@ -22,7 +22,7 @@
 LEFT = 1280
 MAIN = 1920
 TAIL = D - MAIN
-EARLY = 896
+EARLY = 1024
 ORDER = (0, 1, 2, 7, 6, 3, 4, 5)
 
 HERE, NEXT, PREV, FAR = 0, 1, 2, 3
@@ -386,6 +386,27 @@
         def _(n):
             down(start, rows, pl.ds(pl.multiple_of(n * 512, 512), 512))
 
+    groups = ((1, PREV), (0, HERE))
+    phases = (
+        (pl.ds(0, EARLY), pl.ds(LEFT, EARLY)),
+        (pl.ds(EARLY, LEFT - EARLY), pl.ds(LEFT + EARLY, LEFT - EARLY)),
+    )
+
+    def yb(b, h, a, n, cols):
+        return ys.at[pl.ds(row(b, h, a), n * HALF), cols]
+
+    def spot(g):
+        return pl.ds(2 * g * HALF, 2 * HALF)
+
+    reduce = [{} for _ in streams]
+
+    def direct(g, a):
+        for i in four:
+            h, cols, near, next_, af, ab, bf, bb = streams[i]
+            reduce[i]["behind", g] = copies.start(
+                yb(near, h, a, 2, cols), behind.at[h, spot(g), cols], bb
+            )
+
     for i in four:
         pass_b(i, streams[i][2])
     for i in four:
@@ -414,6 +435,7 @@
         for i in four:
             gather[i]["b", streams[i][3], a].wait_recv()
     routed(0, 12 * HALF)
+    direct(0, HERE)
     to_twin[1].wait_recv()
     to_twin[2].wait_recv()
     shared(PREV)
@@ -424,28 +446,6 @@
     ring[3].wait_recv()
     to_twin.append(copies.start(sx(FAR, 0), sx(FAR, 1), twin))
 
-    groups = ((1, PREV), (0, HERE))
-    phases = (
-        (pl.ds(0, EARLY), pl.ds(LEFT, EARLY)),
-        (pl.ds(EARLY, LEFT - EARLY), pl.ds(LEFT + EARLY, LEFT - EARLY)),
-    )
-
-    def yb(b, h, a, n, cols):
-        return ys.at[pl.ds(row(b, h, a), n * HALF), cols]
-
-    def spot(g):
-        return pl.ds(2 * g * HALF, 2 * HALF)
-
-    reduce = [{} for _ in streams]
-
-    def direct(g, a):
-        for i in four:
-            h, cols, near, next_, af, ab, bf, bb = streams[i]
-            reduce[i]["behind", g] = copies.start(
-                yb(near, h, a, 2, cols), behind.at[h, spot(g), cols], bb
-            )
-
-    direct(0, HERE)
     for a in (PREV, FAR):
         for i in four:
             gather[i]["b", streams[i][3], a].wait_recv()

time: 110 us -> 109 us (level)
  no operation moved by 1% of the time
where the time goes in v5:
time: 109 us
  Pallas kernels  107 us (98%)
  local copies, waits for them, and re-layouts  1.97 us (2%)
    pallas_call x1, Pallas kernels, local(): pl.pallas_call(kernel, out_shape=jax.ShapeDtypeStruct((TOK, D), BF16), in...  107 us

profile of v5, /device:TPU:1, one launch (start us, length us, event | category | flops | bytes accessed | tf_op | source)
XLA Modules:
  0.0 109.2 jit_solution(4809664350499960113)
XLA Ops:
  0.0 107.2 %shard_map.109 = bf16[128,2560]{1,0:T(8,128)(2,1)} custom-call(s32[6,128]{1,0:T(8,128)} %bitcast.4, s32[3,128]{1,0:T(4,128)} %bitcast.6, s32[3,128]{1,0:T(4,128)} %bitcast.7, f32[6,128]{1,0:T(8,128)} %bitcast.5, bf16[128,2560]{1,0:T(8,128)(2,1)} %tok_hbm.1, bf16[3,2560,128]{2,1,0:T(8,128)(2,1)} %wg_hbm.1, bf16[3,2560,128]{2,1,0:T(8,128)(2,1)} %wu_hbm.1, ...), custom_call_target="tpu_custom_call" | custom-call | flops 13100000256 | bytes 12000000 | tf_op jit(solution)/shard_map/pallas_call | solution.py:618
  107.2 2.0 %copy.13 = bf16[128,2560]{1,0:T(8,128)(2,1)} copy(bf16[128,2560]{1,0:T(8,128)(2,1)} %shard_map.109) | data formatting | bytes 1310720
